TPU v7x, 128 devices: a whole 4x4x4 slice. The times are simulated.
128 devices in a mesh: wide: 32 (over z, x, core), narrow: 4 (over y).
Axes of the slice: x: 4, y: 4, z: 4, core: 2. Of those that a mesh axis runs over, the one named last changes fastest.
Arguments:
- flow_field: bfloat16 [256, 64, 16, 512], P('wide', 'narrow'), may hold values from -48 to 48
- fluid_mask: int32 [256, 64, 16], P('wide', 'narrow'), may hold values 0 or 1
- conv_weight: float32 [27, 512], replicated, may hold values from -1 to 1
- latents: bfloat16 [1024, 512], replicated, may hold values from -6 to 6
- w_query1: bfloat16 [512, 512], replicated, may hold values from -0.25 to 0.25
- w_key1: bfloat16 [512, 512], replicated, may hold values from -0.25 to 0.25
- w_value1: bfloat16 [512, 512], replicated, may hold values from -0.25 to 0.25
- w_out1: bfloat16 [512, 512], replicated, may hold values from -0.25 to 0.25
- w_query2: bfloat16 [512, 512], replicated, may hold values from -0.25 to 0.25
- w_key2: bfloat16 [512, 512], replicated, may hold values from -0.25 to 0.25
- w_value2: bfloat16 [512, 512], replicated, may hold values from -0.25 to 0.25
- w_out2: bfloat16 [512, 512], replicated, may hold values from -0.25 to 0.25
Outputs:
- updated_field: float32 [256, 64, 16, 512], P('wide', 'narrow')
All inputs are finite; a program needn't handle non-finite values. No bound on the sum of `fluid_mask` on one device may be relied on, other than what follows from the above.
Results may differ from a plain program's by a relative error of at most 0.035.
The roundings to bfloat16 on the way count: a program that leaves them out, or rounds other values in their place, can miss the bound.
Values may be sent and summed in bfloat16 or wider, within the bound.
A program may use at most 192 MiB of HBM per device.

v0:
```python
import math

import jax
import jax.numpy as jnp
from jax import lax
from jax.sharding import PartitionSpec as P

HEADS = 8


def padded_2(cells, sides, width):
    for axis, dim in sides:
        count = lax.axis_size(axis)
        ends = count - 1
        head = lax.slice_in_dim(cells, 0, width, axis=dim)
        tail = lax.slice_in_dim(cells, cells.shape[dim] - width, cells.shape[dim], axis=dim)
        cells = jnp.concatenate(
            [
                lax.ppermute(tail, axis, [(i, (i + 1) % count) for i in range(ends)]),
                cells,
                lax.ppermute(head, axis, [((i + 1) % count, i) for i in range(ends)]),
            ],
            axis=dim,
        )
    return cells


def head_block(matrix, head_index, head_size):
    return matrix[:, head_index * head_size : (head_index + 1) * head_size]


def pair_scores(queries, key_rows, head_size):
    factor = 1.8 / math.sqrt(head_size)
    return factor * lax.dot_general(
        queries, key_rows, (((1,), (1,)), ((), ())), preferred_element_type=jnp.float32
    )


def project(row_block, weight):
    return jnp.dot(row_block, weight, preferred_element_type=jnp.float32).astype(jnp.bfloat16)


def exact_dot(weights, values_block):
    return jnp.dot(
        weights, values_block, precision=lax.Precision.HIGHEST, preferred_element_type=jnp.float32
    )


def update_state(summed, totals, state_rows, w_out1, head_count):
    row_count, model_width = summed.shape
    shaped = summed.reshape(row_count, head_count, model_width // head_count) / totals[:, :, None]
    read_rows = shaped.reshape(row_count, model_width).astype(jnp.bfloat16)
    updated = state_rows.astype(jnp.float32) + jnp.dot(
        read_rows, w_out1, preferred_element_type=jnp.float32
    )
    return updated.astype(jnp.bfloat16)


def per_device(
    flow_field,
    fluid_mask,
    conv_weight,
    latents,
    w_query1,
    w_key1,
    w_value1,
    w_out1,
    w_query2,
    w_key2,
    w_value2,
    w_out2,
):
    size_x, size_y, size_z, model_width = flow_field.shape
    head_count = HEADS
    head_size = model_width // head_count
    masked = flow_field * fluid_mask[:, :, :, None].astype(jnp.bfloat16)
    padded = padded_2(masked, (("wide", 0), ("narrow", 1)), 1)
    padded = jnp.pad(padded, ((0, 0), (0, 0), (1, 1), (0, 0)))
    stencil = masked.astype(jnp.float32)
    for offset_x in range(3):
        for offset_y in range(3):
            for offset_z in range(3):
                window = padded[
                    offset_x : offset_x + size_x,
                    offset_y : offset_y + size_y,
                    offset_z : offset_z + size_z,
                ]
                stencil = (
                    stencil
                    + window.astype(jnp.float32)
                    * conv_weight[9 * offset_x + 3 * offset_y + offset_z]
                )
    cell_count = size_x * size_y * size_z
    mixed_cells = stencil.astype(jnp.bfloat16).reshape(cell_count, model_width)
    flat_masked = masked.reshape(cell_count, model_width)
    keys1 = project(mixed_cells, w_key1)
    values1 = project(mixed_cells, w_value1)
    values_wide = values1.astype(jnp.float32)
    queries1 = project(latents, w_query1)
    local_top = jnp.stack(
        [
            jnp.max(
                pair_scores(
                    head_block(queries1, head_index, head_size),
                    head_block(keys1, head_index, head_size),
                    head_size,
                ),
                axis=1,
            )
            for head_index in range(head_count)
        ],
        axis=1,
    )
    top1 = lax.pmax(local_top.astype(jnp.bfloat16), ("wide", "narrow")).astype(local_top.dtype)
    sums_list = []
    totals_list = []
    for head_index in range(head_count):
        scores = pair_scores(
            head_block(queries1, head_index, head_size),
            head_block(keys1, head_index, head_size),
            head_size,
        )
        weights = jnp.exp(scores - top1[:, head_index : head_index + 1])
        totals_list.append(jnp.sum(weights, axis=1))
        sums_list.append(exact_dot(weights, head_block(values_wide, head_index, head_size)))
    summed1 = jnp.concatenate(sums_list, axis=1)
    totals1 = jnp.stack(totals_list, axis=1)
    summed, totals = lax.psum((summed1, totals1), ("wide", "narrow"))
    latent_state = update_state(summed, totals, latents, w_out1, head_count)
    keys2 = project(latent_state, w_key2)
    values2 = project(latent_state, w_value2)
    queries2 = project(mixed_cells, w_query2)
    read_heads = []
    for head_index in range(head_count):
        scores = pair_scores(
            head_block(queries2, head_index, head_size),
            head_block(keys2, head_index, head_size),
            head_size,
        )
        top2 = jnp.max(scores, axis=1, keepdims=True)
        weights = jnp.exp(scores - top2)
        totals = jnp.sum(weights, axis=1, keepdims=True)
        summed = jnp.dot(
            weights.astype(jnp.bfloat16),
            head_block(values2, head_index, head_size),
            preferred_element_type=jnp.float32,
        )
        read_heads.append(summed / totals)
    read2 = jnp.concatenate(read_heads, axis=1).astype(jnp.bfloat16)
    result = flat_masked.astype(jnp.float32) + jnp.dot(
        read2, w_out2, preferred_element_type=jnp.float32
    )
    return result.reshape(size_x, size_y, size_z, model_width)


def solution(mesh):
    return jax.shard_map(
        per_device,
        mesh=mesh,
        in_specs=(
            P("wide", "narrow", None, None),
            P("wide", "narrow", None),
            P(),
            P(),
            P(),
            P(),
            P(),
            P(),
            P(),
            P(),
            P(),
            P(),
        ),
        out_specs=P("wide", "narrow", None, None),
        check_vma=False,
    )
```

profile of v0, /device:TPU:1, one launch (start us, length us, event | category | flops | bytes accessed | tf_op | source)
XLA Modules:
  0.0 483.6 jit_solution(9292404089981277964)
XLA Ops:
  7.6 1.9 broadcast_multiply_fusion
  9.6 4.5 collective-permute-start
  14.1 1.9 collective-permute-start.1
  17.4 4.4 collective-permute-done.1
  21.8 3.2 collective-permute-start.2
  27.3 3.8 collective-permute-done.3
  32.0 2.8 select_maximum_fusion
  34.8 16.1 %add_convert_fusion = bf16[8,16,16,512]{3,2,1,0:T(8,128)(2,1)S(1)} fusion(bf16[8,16,16,512]{3,2,1,0:T(8,128)(2,1)S(1)} %broadcast_multiply_fusion, bf16[10,18,18,512]{3,2,1,0:T(8,128)(2,1)S(1)} %select_maximum_fusion, bf16[10,17,16,512]{3,2,1,0:T(8,128)(2,1)S(1)} %get-tuple-element.6, bf16[1,16,16,512]{3,2,1,0:T(8,128)(2,1)S(1)} %collective-permute-done.1, ...), kind=kLoop, calls=%fused_computation.115 | loop fusion | flops 88080384 | bytes 55105536 | tf_op jit(solution)/shard_map/convert_element_type | solution.py:94
  52.2 4.5 multiply_reduce_fusion.15
  56.7 4.5 multiply_reduce_fusion.14
  61.2 4.5 multiply_reduce_fusion.13
  65.7 4.5 multiply_reduce_fusion.12
  70.2 4.5 multiply_reduce_fusion.11
  74.7 4.5 multiply_reduce_fusion.10
  79.2 4.5 multiply_reduce_fusion.9
  83.6 4.5 multiply_reduce_fusion.8
  88.3 68.1 %pmax.7 = bf16[1024,8]{0,1:T(8,128)(2,1)S(1)} all-reduce(bf16[1024,8]{0,1:T(8,128)(2,1)S(1)} %stack.71), channel_id=1, replica_groups=mesh['wide'=32,'narrow'=4] {'wide','narrow'}, use_global_device_ids=true, to_apply=%region_8.9 | all-reduce | flops 8192 | bytes 32768 | tf_op jit(solution)/shard_map/pmax | solution.py:114
  157.7 5.4 %fusion.5 = f32[1024]{0:T(1024)S(1)} fusion(f32[1024,2048]{1,0:T(8,128)} %get-tuple-element.51, f32[1024]{0:T(1024)S(1)} %bitcast.100), kind=kLoop, calls=%fused_computation.39 | loop fusion | flops 6290432 | bytes 8396800 | tf_op jit(solution)/shard_map/reduce_sum | solution.py:124
  163.1 5.5 %fusion.142 = f32[1024,512]{0,1:T(8,128)S(1)} fusion(f32[1024,2048]{1,0:T(8,128)S(1)} %bitcast.68, f32[1024]{0:T(1024)S(1)} %bitcast.86, bf16[2048,512]{0,1:T(8,128)(2,1)S(1)} %convolution_convert_fusion), kind=kOutput, calls=%fused_computation.152 | convolution fusion | flops 1614807040 | bytes 8916992 | tf_op jit(solution)/shard_map/dot_general | solution.py:44
  168.7 5.5 %fusion.141 = f32[1024,512]{0,1:T(8,128)S(1)} fusion(f32[1024,512]{0,1:T(8,128)S(1)} %fusion.142, f32[1024,2048]{1,0:T(8,128)S(1)} %bitcast.70, f32[1024]{0:T(1024)S(1)} %bitcast.88, bf16[2048,512]{0,1:T(8,128)(2,1)S(1)} %convolution_convert_fusion), kind=kOutput, calls=%fused_computation.151 | convolution fusion | flops 1614807040 | bytes 8916992 | tf_op jit(solution)/shard_map/dot_general | solution.py:44
  174.3 5.7 %fusion.140 = f32[1024,512]{0,1:T(8,128)S(1)} fusion(f32[1024,512]{0,1:T(8,128)S(1)} %fusion.141, f32[1024,2048]{1,0:T(8,128)S(1)} %bitcast.82, f32[1024]{0:T(1024)S(1)} %bitcast.101, bf16[2048,512]{0,1:T(8,128)(2,1)S(1)} %convolution_convert_fusion), kind=kOutput, calls=%fused_computation.150 | convolution fusion | flops 1614807040 | bytes 8916992 | tf_op jit(solution)/shard_map/dot_general | solution.py:44
  180.0 1.9 fusion.7
  182.0 5.5 %fusion.139 = f32[1024,512]{0,1:T(8,128)S(1)} fusion(f32[1024,512]{0,1:T(8,128)S(1)} %fusion.140, f32[1024,2048]{1,0:T(8,128)S(1)} %bitcast.80, f32[1024]{0:T(1024)S(1)} %bitcast.99, bf16[2048,512]{0,1:T(8,128)(2,1)S(1)} %convolution_convert_fusion), kind=kOutput, calls=%fused_computation.149 | convolution fusion | flops 1614807040 | bytes 8916992 | tf_op jit(solution)/shard_map/dot_general | solution.py:44
  187.5 2.1 fusion.9
  189.7 5.5 %fusion.138 = f32[1024,512]{0,1:T(8,128)S(1)} fusion(f32[1024,512]{0,1:T(8,128)S(1)} %fusion.139, f32[1024,2048]{1,0:T(8,128)S(1)} %bitcast.78, f32[1024]{0:T(1024)S(1)} %bitcast.97, bf16[2048,512]{0,1:T(8,128)(2,1)S(1)} %convolution_convert_fusion), kind=kOutput, calls=%fused_computation.148 | convolution fusion | flops 1614807040 | bytes 8916992 | tf_op jit(solution)/shard_map/dot_general | solution.py:44
  195.3 1.9 fusion.11
  197.2 5.5 %fusion.137 = f32[1024,512]{0,1:T(8,128)S(1)} fusion(f32[1024,512]{0,1:T(8,128)S(1)} %fusion.138, f32[1024,2048]{1,0:T(8,128)S(1)} %bitcast.76, f32[1024]{0:T(1024)S(1)} %bitcast.95, bf16[2048,512]{0,1:T(8,128)(2,1)S(1)} %convolution_convert_fusion), kind=kOutput, calls=%fused_computation.147 | convolution fusion | flops 1614807040 | bytes 8916992 | tf_op jit(solution)/shard_map/dot_general | solution.py:44
  202.8 2.3 fusion.13
  205.1 5.5 %fusion.136 = f32[1024,512]{0,1:T(8,128)S(1)} fusion(f32[1024,512]{0,1:T(8,128)S(1)} %fusion.137, f32[1024,2048]{1,0:T(8,128)S(1)} %bitcast.74, f32[1024]{0:T(1024)S(1)} %bitcast.93, bf16[2048,512]{0,1:T(8,128)(2,1)S(1)} %convolution_convert_fusion), kind=kOutput, calls=%fused_computation.146 | convolution fusion | flops 1614807040 | bytes 8916992 | tf_op jit(solution)/shard_map/dot_general | solution.py:44
  210.7 2.1 fusion.15
  212.8 5.5 %fusion.135 = f32[1024,512]{0,1:T(8,128)S(1)} fusion(f32[1024,512]{0,1:T(8,128)S(1)} %fusion.136, f32[1024,2048]{1,0:T(8,128)S(1)} %bitcast.72, f32[1024]{0:T(1024)S(1)} %bitcast.91, bf16[2048,512]{0,1:T(8,128)(2,1)S(1)} %convolution_convert_fusion), kind=kOutput, calls=%fused_computation.145 | convolution fusion | flops 1614807040 | bytes 8916992 | tf_op jit(solution)/shard_map/dot_general | solution.py:44
  219.7 4.4 fusion.3
  224.0 4.6 fusion.1
  228.7 63.9 %psum.15 = f32[1024,8]{0,1:T(8,128)S(1)} all-reduce(f32[1024,8]{0,1:T(8,128)S(1)} %stack.80), channel_id=1, replica_groups=mesh['wide'=32,'narrow'=4] {'wide','narrow'}, use_global_device_ids=true, to_apply=%region_18.19 | all-reduce | flops 8192 | bytes 65536 | tf_op jit(solution)/shard_map/psum | solution.py:128
  292.6 2.9 convolution_convert_fusion.2
  295.5 72.0 %all-reduce.3.cloned.1.call-done = f32[1024,512]{0,1:T(8,128)} async-done(((f32[1024,512]{0,1:T(8,128)}), f32[1024,512]{0,1:T(8,128)}) %all-reduce.3.cloned.1.call-update) | async-done | bytes 2097168 | tf_op jit(solution)/shard_map/psum | solution.py:128
  367.5 1.8 fusion.86
  369.3 2.1 add_convert_fusion.1
  372.2 4.5 multiply_reduce_fusion
  376.7 4.5 multiply_reduce_fusion.1
  381.2 4.5 multiply_reduce_fusion.2
  385.8 4.5 multiply_reduce_fusion.3
  390.3 4.5 multiply_reduce_fusion.4
  394.8 1.3 multiply_reduce_fusion.5
  396.1 1.3 multiply_reduce_fusion.6
  397.4 1.8 multiply_reduce_fusion.7
  400.0 4.8 fusion.31
  404.8 5.9 %fusion.132 = bf16[2048,64]{1,0:T(8,128)(2,1)} fusion(f32[2048,1024]{0,1:T(8,128)} %get-tuple-element.77, f32[2048]{0:T(1024)S(1)} %get-tuple-element.76, f32[2048]{0:T(1024)S(1)} %fusion.31, bf16[1024,512]{0,1:T(8,128)(2,1)S(1)} %convolution_convert_fusion.3), kind=kOutput, calls=%fused_computation.141 | convolution fusion | flops 274989056 | bytes 8798208 | tf_op jit(solution)/shard_map/dot_general | solution.py:143
  410.7 4.8 fusion.29
  415.5 5.9 %fusion.126 = bf16[2048,64]{1,0:T(8,128)(2,1)} fusion(f32[2048,1024]{0,1:T(8,128)} %get-tuple-element.75, f32[2048]{0:T(1024)S(1)} %get-tuple-element.74, f32[2048]{0:T(1024)S(1)} %fusion.29, bf16[1024,512]{0,1:T(8,128)(2,1)S(1)} %convolution_convert_fusion.3), kind=kOutput, calls=%fused_computation.139 | convolution fusion | flops 274989056 | bytes 8798208 | tf_op jit(solution)/shard_map/dot_general | solution.py:143
  421.4 4.8 fusion.27
  426.1 5.9 %fusion.120 = bf16[2048,64]{1,0:T(8,128)(2,1)} fusion(f32[2048,1024]{0,1:T(8,128)} %get-tuple-element.73, f32[2048]{0:T(1024)S(1)} %get-tuple-element.72, f32[2048]{0:T(1024)S(1)} %fusion.27, bf16[1024,512]{0,1:T(8,128)(2,1)S(1)} %convolution_convert_fusion.3), kind=kOutput, calls=%fused_computation.137 | convolution fusion | flops 274989056 | bytes 8798208 | tf_op jit(solution)/shard_map/dot_general | solution.py:143
  432.0 5.0 %fusion.25 = f32[2048]{0:T(1024)S(1)} fusion(f32[2048,1024]{0,1:T(8,128)} %get-tuple-element.71, f32[2048]{0:T(1024)S(1)} %get-tuple-element.70), kind=kLoop, calls=%fused_computation.59 | loop fusion | flops 6289408 | bytes 8404992 | tf_op jit(solution)/shard_map/reduce_sum | solution.py:142
  437.0 5.9 %fusion.114 = bf16[2048,64]{1,0:T(8,128)(2,1)} fusion(f32[2048,1024]{0,1:T(8,128)} %get-tuple-element.71, f32[2048]{0:T(1024)S(1)} %get-tuple-element.70, f32[2048]{0:T(1024)S(1)} %fusion.25, bf16[1024,512]{0,1:T(8,128)(2,1)S(1)} %convolution_convert_fusion.3), kind=kOutput, calls=%fused_computation.135 | convolution fusion | flops 274989056 | bytes 8798208 | tf_op jit(solution)/shard_map/dot_general | solution.py:143
  442.8 4.8 fusion.23
  447.6 5.9 %fusion.108 = bf16[2048,64]{1,0:T(8,128)(2,1)} fusion(f32[2048,1024]{0,1:T(8,128)} %get-tuple-element.69, f32[2048]{0:T(1024)S(1)} %get-tuple-element.68, f32[2048]{0:T(1024)S(1)} %fusion.23, bf16[1024,512]{0,1:T(8,128)(2,1)S(1)} %convolution_convert_fusion.3), kind=kOutput, calls=%fused_computation.133 | convolution fusion | flops 274989056 | bytes 8798208 | tf_op jit(solution)/shard_map/dot_general | solution.py:143
  453.5 1.4 fusion.21
  454.9 2.5 fusion.102
  457.4 1.4 fusion.19
  458.8 2.5 fusion.96
  461.2 1.4 fusion.17
  462.6 2.5 fusion.90
  465.1 6.6 %concatenate.36 = bf16[2048,512]{1,0:T(8,128)(2,1)} concatenate(bf16[2048,64]{1,0:T(8,128)(2,1)} %fusion.90, bf16[2048,64]{1,0:T(8,128)(2,1)} %fusion.96, bf16[2048,64]{1,0:T(8,128)(2,1)} %fusion.102, bf16[2048,64]{1,0:T(8,128)(2,1)} %fusion.108, bf16[2048,64]{1,0:T(8,128)(2,1)} %fusion.114, bf16[2048,64]{1,0:T(8,128)(2,1)} %fusion.120, bf16[2048,64]{1,0:T(8,128)(2,1)} %fusion.126, ...), dimensions={1} | concatenate | bytes 4194304 | tf_op jit(solution)/shard_map/concatenate | solution.py:149
  471.7 4.9 %bitcast_add_fusion = f32[2048,512]{1,0:T(8,128)} fusion(bf16[8,16,16,512]{3,2,1,0:T(8,128)(2,1)S(1)} %copy-done.3, bf16[2048,512]{1,0:T(8,128)(2,1)} %concatenate.36, bf16[512,512]{1,0:T(8,128)(2,1)S(1)} %copy-done.6), kind=kOutput, calls=%fused_computation.82 | convolution fusion | flops 1075838976 | bytes 8912896 | tf_op jit(solution)/shard_map/dot_general | solution.py:150
  (95 shorter events, 11.3 us)
Async XLA Ops:
  6.5 44.4 %copy-start = (bf16[512,512]{1,0:T(8,128)(2,1)S(1)}, bf16[512,512]{1,0:T(8,128)(2,1)}, u32[]{:S(2)}) copy-start(bf16[512,512]{1,0:T(8,128)(2,1)} %param.17) | copy-start | bytes 1572868
  6.5 9.5 %copy-start.7 = (f32[27,512]{1,0:T(8,128)S(1)}, f32[27,512]{1,0:T(8,128)}, u32[]{:S(2)}) copy-start(f32[27,512]{1,0:T(8,128)} %param.14) | copy-start | bytes 165892
  6.5 9.5 %copy-start.8 = (bf16[1024,512]{1,0:T(8,128)(2,1)S(1)}, bf16[1024,512]{1,0:T(8,128)(2,1)}, u32[]{:S(2)}) copy-start(bf16[1024,512]{1,0:T(8,128)(2,1)} %param.15) | copy-start | bytes 3145732
  6.5 9.5 %copy-start.9 = (bf16[512,512]{1,0:T(8,128)(2,1)S(1)}, bf16[512,512]{1,0:T(8,128)(2,1)}, u32[]{:S(2)}) copy-start(bf16[512,512]{1,0:T(8,128)(2,1)} %param.16) | copy-start | bytes 1572868
  6.5 360.9 %all-reduce.3.cloned.1.call-start = ((), (), s32[]{:S(2)}) async-start(), calls=%async_computation | async-start | bytes 4194304 | tf_op jit(solution)/shard_map/psum | solution.py:128
  9.5 25.3 %copy-start.2 = (bf16[8,16,16,512]{3,2,1,0:T(8,128)(2,1)}, bf16[8,16,16,512]{3,2,1,0:T(8,128)(2,1)S(1)}, u32[]{:S(2)}) copy-start(bf16[8,16,16,512]{3,2,1,0:T(8,128)(2,1)S(1)} %broadcast_multiply_fusion) | copy-start | bytes 6291460
  9.6 7.8 %collective-permute-start = (bf16[1,16,16,512]{3,2,1,0:T(8,128)(2,1)S(1)}, bf16[1,16,16,512]{3,2,1,0:T(8,128)(2,1)S(1)}, u32[]{:S(2)}, u32[]{:S(2)}) collective-permute-start(bf16[1,16,16,512]{3,2,1,0:T(8,128)(2,1)S(1)} %get-tuple-element.9), channel_id=1, source_target_pairs={{0,4},{4,8},{8,12},{12,16},{16,20},{20,24},{24,28},{28,32},{32,36}... | collective-permute-start | bytes 786440 | tf_op jit(solution)/shard_map/ppermute | solution.py:19
  14.1 7.7 %collective-permute-start.1 = (bf16[1,16,16,512]{3,2,1,0:T(8,128)(2,1)S(1)}, bf16[1,16,16,512]{3,2,1,0:T(8,128)(2,1)S(1)}, u32[]{:S(2)}, u32[]{:S(2)}) collective-permute-start(bf16[1,16,16,512]{3,2,1,0:T(8,128)(2,1)S(1)} %get-tuple-element.10), channel_id=1, source_target_pairs={{4,0},{8,4},{12,8},{16,12},{20,16},{24,20},{28,24},{32,28},{36,32}... | collective-permute-start | bytes 786440 | tf_op jit(solution)/shard_map/ppermute | solution.py:21
  21.8 5.5 %collective-permute-start.2 = (bf16[10,1,16,512]{3,2,1,0:T(8,128)(2,1)S(1)}, bf16[10,1,16,512]{3,2,1,0:T(8,128)(2,1)S(1)}, u32[]{:S(2)}, u32[]{:S(2)}) collective-permute-start(bf16[10,1,16,512]{3,2,1,0:T(8,128)(2,1)S(1)} %get-tuple-element.7), channel_id=1, source_target_pairs={{0,1},{1,2},{2,3},{4,5},{5,6},{6,7},{8,9},{9,10},{10,11},{12,13},{... | collective-permute-start | bytes 491528 | tf_op jit(solution)/shard_map/ppermute | solution.py:19
  25.0 6.1 %collective-permute-start.3 = (bf16[10,1,16,512]{3,2,1,0:T(8,128)(2,1)S(1)}, bf16[10,1,16,512]{3,2,1,0:T(8,128)(2,1)S(1)}, u32[]{:S(2)}, u32[]{:S(2)}) collective-permute-start(bf16[10,1,16,512]{3,2,1,0:T(8,128)(2,1)S(1)} %get-tuple-element.8), channel_id=1, source_target_pairs={{1,0},{2,1},{3,2},{5,4},{6,5},{7,6},{9,8},{10,9},{11,10},{13,12},{... | collective-permute-start | bytes 491528 | tf_op jit(solution)/shard_map/ppermute | solution.py:21
  50.9 105.5 %copy-start.5 = (bf16[8,16,16,512]{3,2,1,0:T(8,128)(2,1)}, bf16[8,16,16,512]{3,2,1,0:T(8,128)(2,1)S(1)}, u32[]{:S(2)}) copy-start(bf16[8,16,16,512]{3,2,1,0:T(8,128)(2,1)S(1)} %add_convert_fusion) | copy-start | bytes 6291460
  83.6 72.7 %copy-start.10 = (bf16[512,512]{1,0:T(8,128)(2,1)S(1)}, bf16[512,512]{1,0:T(8,128)(2,1)}, u32[]{:S(2)}) copy-start(bf16[512,512]{1,0:T(8,128)(2,1)} %param.18) | copy-start | bytes 1572868
  156.3 6.8 %slice-start = ((s8[8388608]{0:T(1024)(128)(4,1)}), s8[4194304]{0:T(1024)(128)(4,1)S(1)}, s32[]{:S(2)}) async-start(s8[8388608]{0:T(1024)(128)(4,1)} %bitcast.67), calls=%async_computation.1 | async-start | bytes 8388608
  156.4 6.7 %slice-start.1 = ((s8[8388608]{0:T(1024)(128)(4,1)}), s8[4194304]{0:T(1024)(128)(4,1)S(1)}, s32[]{:S(2)}) async-start(s8[8388608]{0:T(1024)(128)(4,1)} %bitcast.67), calls=%async_computation.2 | async-start | bytes 8388608
  157.7 11.0 %slice-start.2 = ((s8[8388608]{0:T(1024)(128)(4,1)}), s8[4194304]{0:T(1024)(128)(4,1)S(1)}, s32[]{:S(2)}) async-start(s8[8388608]{0:T(1024)(128)(4,1)} %bitcast.69), calls=%async_computation.3 | async-start | bytes 8388608
  157.7 16.5 %slice-start.14 = ((s8[8388608]{0:T(1024)(128)(4,1)}), s8[4194304]{0:T(1024)(128)(4,1)S(1)}, s32[]{:S(2)}) async-start(s8[8388608]{0:T(1024)(128)(4,1)} %bitcast.81), calls=%async_computation.15 | async-start | bytes 8388608
  163.1 5.6 %slice-start.3 = ((s8[8388608]{0:T(1024)(128)(4,1)}), s8[4194304]{0:T(1024)(128)(4,1)S(1)}, s32[]{:S(2)}) async-start(s8[8388608]{0:T(1024)(128)(4,1)} %bitcast.69), calls=%async_computation.4 | async-start | bytes 8388608
  163.1 11.1 %slice-start.15 = ((s8[8388608]{0:T(1024)(128)(4,1)}), s8[4194304]{0:T(1024)(128)(4,1)S(1)}, s32[]{:S(2)}) async-start(s8[8388608]{0:T(1024)(128)(4,1)} %bitcast.81), calls=%async_computation.16 | async-start | bytes 8388608
  168.7 11.3 %slice-start.12 = ((s8[8388608]{0:T(1024)(128)(4,1)}), s8[4194304]{0:T(1024)(128)(4,1)S(1)}, s32[]{:S(2)}) async-start(s8[8388608]{0:T(1024)(128)(4,1)} %bitcast.79), calls=%async_computation.13 | async-start | bytes 8388608
  174.3 5.7 %slice-start.13 = ((s8[8388608]{0:T(1024)(128)(4,1)}), s8[4194304]{0:T(1024)(128)(4,1)S(1)}, s32[]{:S(2)}) async-start(s8[8388608]{0:T(1024)(128)(4,1)} %bitcast.79), calls=%async_computation.14 | async-start | bytes 8388608
  180.0 7.5 %slice-start.10 = ((s8[8388608]{0:T(1024)(128)(4,1)}), s8[4194304]{0:T(1024)(128)(4,1)S(1)}, s32[]{:S(2)}) async-start(s8[8388608]{0:T(1024)(128)(4,1)} %bitcast.77), calls=%async_computation.11 | async-start | bytes 8388608
  182.0 5.6 %slice-start.11 = ((s8[8388608]{0:T(1024)(128)(4,1)}), s8[4194304]{0:T(1024)(128)(4,1)S(1)}, s32[]{:S(2)}) async-start(s8[8388608]{0:T(1024)(128)(4,1)} %bitcast.77), calls=%async_computation.12 | async-start | bytes 8388608
  187.5 7.7 %slice-start.8 = ((s8[8388608]{0:T(1024)(128)(4,1)}), s8[4194304]{0:T(1024)(128)(4,1)S(1)}, s32[]{:S(2)}) async-start(s8[8388608]{0:T(1024)(128)(4,1)} %bitcast.75), calls=%async_computation.9 | async-start | bytes 8388608
  189.7 5.6 %slice-start.9 = ((s8[8388608]{0:T(1024)(128)(4,1)}), s8[4194304]{0:T(1024)(128)(4,1)S(1)}, s32[]{:S(2)}) async-start(s8[8388608]{0:T(1024)(128)(4,1)} %bitcast.75), calls=%async_computation.10 | async-start | bytes 8388608
  195.3 7.5 %slice-start.6 = ((s8[8388608]{0:T(1024)(128)(4,1)}), s8[4194304]{0:T(1024)(128)(4,1)S(1)}, s32[]{:S(2)}) async-start(s8[8388608]{0:T(1024)(128)(4,1)} %bitcast.73), calls=%async_computation.7 | async-start | bytes 8388608
  197.2 5.6 %slice-start.7 = ((s8[8388608]{0:T(1024)(128)(4,1)}), s8[4194304]{0:T(1024)(128)(4,1)S(1)}, s32[]{:S(2)}) async-start(s8[8388608]{0:T(1024)(128)(4,1)} %bitcast.73), calls=%async_computation.8 | async-start | bytes 8388608
  202.8 7.9 %slice-start.4 = ((s8[8388608]{0:T(1024)(128)(4,1)}), s8[4194304]{0:T(1024)(128)(4,1)S(1)}, s32[]{:S(2)}) async-start(s8[8388608]{0:T(1024)(128)(4,1)} %bitcast.71), calls=%async_computation.5 | async-start | bytes 8388608
  205.1 5.6 %slice-start.5 = ((s8[8388608]{0:T(1024)(128)(4,1)}), s8[4194304]{0:T(1024)(128)(4,1)S(1)}, s32[]{:S(2)}) async-start(s8[8388608]{0:T(1024)(128)(4,1)} %bitcast.71), calls=%async_computation.6 | async-start | bytes 8388608
  218.3 1.3 copy-start.4
  224.0 68.6 %copy-start.11 = (bf16[512,512]{1,0:T(8,128)(2,1)S(1)}, bf16[512,512]{1,0:T(8,128)(2,1)}, u32[]{:S(2)}) copy-start(bf16[512,512]{1,0:T(8,128)(2,1)} %param.20) | copy-start | bytes 1572868
  295.5 76.0 %copy-start.12 = (bf16[512,512]{1,0:T(8,128)(2,1)S(1)}, bf16[512,512]{1,0:T(8,128)(2,1)}, u32[]{:S(2)}) copy-start(bf16[512,512]{1,0:T(8,128)(2,1)} %param.21) | copy-start | bytes 1572868
  397.4 1.8 copy-start.13
  465.1 6.6 %copy-start.3 = (bf16[8,16,16,512]{3,2,1,0:T(8,128)(2,1)S(1)}, bf16[8,16,16,512]{3,2,1,0:T(8,128)(2,1)}, u32[]{:S(2)}) copy-start(bf16[8,16,16,512]{3,2,1,0:T(8,128)(2,1)} %copy-done.2) | copy-start | bytes 6291460
  465.1 6.6 %copy-start.6 = (bf16[512,512]{1,0:T(8,128)(2,1)S(1)}, bf16[512,512]{1,0:T(8,128)(2,1)}, u32[]{:S(2)}) copy-start(bf16[512,512]{1,0:T(8,128)(2,1)} %param.23) | copy-start | bytes 1572868
  465.1 11.5 %copy-start.1 = (bf16[512,512]{1,0:T(8,128)(2,1)S(1)}, bf16[512,512]{1,0:T(8,128)(2,1)}, u32[]{:S(2)}) copy-start(bf16[512,512]{1,0:T(8,128)(2,1)} %param.17) | copy-start | bytes 1572868
Sparse Core Ops, SparseCore 0:
  219.8 147.6 all-reduce.2
where the time goes:
time: 489 us; the launch traced here: 484 us
  matrix products  159 us (33%)
  blocking collectives  132 us (27%)
  waiting for transfers between devices  81.6 us (17%)
  other arithmetic  77.7 us (16%)
  between operations  14.3 us (3%)
  starting transfers between devices  11 us (2%)
  local copies, waits for them, and re-layouts  8.31 us (2%)
    psum x1, waiting for transfers between devices, per_device(): summed, totals = lax.psum((summed1, totals1), ('wide', 'narrow'))  72 us
    pmax x1, blocking collectives, per_device(): lax.pmax(local_top.astype(jnp.bfloat16), ('wide', 'narrow'))  68.1 us
    psum x1, blocking collectives, per_device(): summed, totals = lax.psum((summed1, totals1), ('wide', 'narrow'))  63.9 us
    dot_general x16, matrix products, pair_scores(): lax.dot_general(queries, key_rows, (((1,), (1,)), ((), ())), preferred_el...  62.9 us
    dot_general x8, matrix products, exact_dot(): jnp.dot(weights, values_block, precision=lax.Precision.HIGHEST, preferred...  44.4 us
    dot_general x8, matrix products, per_device(): jnp.dot(weights.astype(jnp.bfloat16), head_block(values2, head_index, hea...  36.8 us
    reduce_sum x8, other arithmetic, per_device(): totals = jnp.sum(weights, axis=1, keepdims=True)  28.3 us
    reduce_sum x8, other arithmetic, per_device(): totals_list.append(jnp.sum(weights, axis=1))  24.8 us
  transfers between devices with their start and end apart: 5, of which 5 were waited for; matrix products, arithmetic and copies ran while one was open for 3% of the time, Pallas kernels for 0%

commit v1 on v0

v1 whole, which is shorter than its diff:
```python
import functools
import math

import jax
import jax.numpy as jnp
from jax import lax
from jax.experimental import pallas as pl
from jax.experimental.pallas import tpu as pltpu
from jax.sharding import PartitionSpec as P

HEADS = 8
MESH = pl.DeviceIdType.MESH
F32 = jnp.float32
BF16 = jnp.bfloat16


def dot(a, b):
    return jnp.dot(a, b, preferred_element_type=F32)


def dot_t(a, b):
    return lax.dot_general(a, b, (((1,), (1,)), ((), ())), preferred_element_type=F32)


def vmem():
    return pl.BlockSpec(memory_space=pltpu.VMEM)


def stencil_kernel(
    cells, conv, latents, w_q1, w_k1, w_v1, w_q2,
    q1, k1, v1, q2,
    x_side, y_side, corner, pad, mixed, send_sem, recv_sem,
):
    size_x, size_y, size_z, width = cells.shape
    wide, narrow = lax.axis_index("wide"), lax.axis_index("narrow")
    wides, narrows = lax.axis_size("wide"), lax.axis_size("narrow")

    def at(step_x, step_y):
        return (lax.rem(wide + step_x + wides, wides), lax.rem(narrow + step_y + narrows, narrows))

    steps = [(1, 0), (-1, 0), (0, 1), (0, -1), (1, 1), (1, -1), (-1, 1), (-1, -1)]
    barrier = pltpu.get_barrier_semaphore()
    for step in steps:
        pl.semaphore_signal(barrier, inc=1, device_id=at(*step), device_id_type=MESH)
    pl.semaphore_wait(barrier, len(steps))

    copies = []
    for index, (step_x, step_y) in enumerate(steps):
        from_x = size_x - 1 if step_x == 1 else 0
        from_y = size_y - 1 if step_y == 1 else 0
        low_x = 0 if step_x == 1 else 1
        low_y = 0 if step_y == 1 else 1
        if step_y == 0:
            source, target = cells.at[from_x], x_side.at[low_x]
        elif step_x == 0:
            source, target = cells.at[:, from_y], y_side.at[low_y]
        else:
            source, target = cells.at[from_x, from_y], corner.at[low_x, low_y]
        copy = pltpu.make_async_remote_copy(
            src_ref=source, dst_ref=target, send_sem=send_sem.at[index], recv_sem=recv_sem.at[index],
            device_id=at(step_x, step_y), device_id_type=MESH,
        )
        copy.start()
        copies.append(copy)

    q1[...] = dot(latents[...], w_q1[...]).astype(BF16)

    def widen(x, carry):
        pad[x + 1, 1 : size_y + 1] = cells[x].astype(F32)
        return carry

    lax.fori_loop(0, size_x, widen, 0)
    for copy in copies:
        copy.wait()
    for low in range(2):
        keep_x = (wide > 0) if low == 0 else (wide < wides - 1)
        keep_y = (narrow > 0) if low == 0 else (narrow < narrows - 1)
        pad[low * (size_x + 1), 1 : size_y + 1] = jnp.where(keep_x, x_side[low].astype(F32), 0.0)
        pad[1 : size_x + 1, low * (size_y + 1)] = jnp.where(keep_y, y_side[low].astype(F32), 0.0)
        for low_y in range(2):
            keep = jnp.logical_and(keep_x, (narrow > 0) if low_y == 0 else (narrow < narrows - 1))
            pad[low * (size_x + 1), low_y * (size_y + 1)] = jnp.where(keep, corner[low, low_y].astype(F32), 0.0)

    level = lax.broadcasted_iota(jnp.int32, (size_z, 128), 0)

    def plane(x, carry):
        for column in range(width // 128):
            lanes = slice(column * 128, column * 128 + 128)
            taps = [conv[tap : tap + 1, lanes] for tap in range(27)]
            for y in range(size_y):
                sums = [None, None, None]
                for a in range(3):
                    for b in range(3):
                        value = pad[x + a, y + b, :, lanes]
                        if a == 1 and b == 1:
                            centre = value
                        for c in range(3):
                            term = value * taps[9 * a + 3 * b + c]
                            sums[c] = term if sums[c] is None else sums[c] + term
                below = jnp.where(level == 0, 0.0, pltpu.roll(sums[0], 1, 0))
                above = jnp.where(level == size_z - 1, 0.0, pltpu.roll(sums[2], size_z - 1, 0))
                total = (centre + sums[1]) + (below + above)
                start = pl.multiple_of((x * size_y + y) * size_z, size_z)
                mixed[pl.ds(start, size_z), lanes] = total.astype(BF16)
        rows = pl.ds(pl.multiple_of(x * size_y * size_z, size_y * size_z), size_y * size_z)
        block = mixed[rows, :]
        k1[rows, :] = dot(block, w_k1[...]).astype(BF16)
        v1[rows, :] = dot(block, w_v1[...]).astype(BF16)
        q2[rows, :] = dot(block, w_q2[...]).astype(BF16)
        return carry

    lax.fori_loop(0, size_x, plane, 0)


def stencil_call(cells, conv, latents, w_q1, w_k1, w_v1, w_q2):
    size_x, size_y, size_z, width = cells.shape
    count = size_x * size_y * size_z
    rows = jax.ShapeDtypeStruct((count, width), BF16)
    return pl.pallas_call(
        stencil_kernel,
        out_shape=(jax.ShapeDtypeStruct(latents.shape, BF16), rows, rows, rows),
        in_specs=[vmem()] * 7,
        out_specs=[vmem()] * 4,
        scratch_shapes=[
            pltpu.VMEM((2, size_y, size_z, width), BF16),
            pltpu.VMEM((2, size_x, size_z, width), BF16),
            pltpu.VMEM((2, 2, size_z, width), BF16),
            pltpu.VMEM((size_x + 2, size_y + 2, size_z, width), F32),
            pltpu.VMEM((count, width), BF16),
            pltpu.SemaphoreType.DMA((8,)),
            pltpu.SemaphoreType.DMA((8,)),
        ],
        compiler_params=pltpu.CompilerParams(
            collective_id=0, has_side_effects=True, vmem_limit_bytes=56 * 2**20
        ),
        name="stencil",
    )(cells, conv, latents, w_q1, w_k1, w_v1, w_q2)


def pipelined(items, scores, weigh, read):
    score, weight, top, out = scores(*items[0]), None, None, {}
    for j in range(len(items) + 1):
        later = scores(*items[j + 1]) if j + 1 < len(items) else None
        fresh = weigh(score) if j < len(items) else (None, None)
        if j > 0:
            out[items[j - 1]] = read(weight, top, *items[j - 1])
        score, (weight, top) = later, fresh
    return out


def latent_kernel(
    scale, block,
    q1, k1, v1, latents, w_o1, w_k2, w_v2,
    k2, v2,
    part, stat, part_in, stat_in, group, group_in, own, gathered, wide_read,
    send_part, recv_part, send_stat, recv_stat, send_group, recv_group,
    send_own, recv_own, send_read, recv_read,
):
    count, width = q1.shape
    cell_count = k1.shape[0]
    pairs = width // 128
    wide, narrow = lax.axis_index("wide"), lax.axis_index("narrow")
    narrows = lax.axis_size("narrow")
    inner = 8
    outer = lax.axis_size("wide") // inner * narrows
    slice_rows = count // inner
    own_rows = slice_rows // outer
    floor = wide // inner
    near = wide - floor * inner
    far = floor * narrows + narrow

    def near_device(step):
        return (floor * inner + lax.rem(near + step, inner), narrow)

    def far_device(step):
        place = lax.rem(far + step, outer)
        return ((place // narrows) * inner + near, lax.rem(place, narrows))

    barrier = pltpu.get_barrier_semaphore()

    def greet_near(step, carry):
        pl.semaphore_signal(barrier, inc=1, device_id=near_device(step), device_id_type=MESH)
        return carry

    def greet_far(step, carry):
        pl.semaphore_signal(barrier, inc=1, device_id=far_device(step), device_id_type=MESH)
        return carry

    lax.fori_loop(1, inner, greet_near, 0)
    lax.fori_loop(1, outer, greet_far, 0)

    lane = lax.broadcasted_iota(jnp.int32, (1, 128), 1)
    level = lax.broadcasted_iota(jnp.int32, (8, 128), 0)

    def attend(pair):
        columns = pl.ds(pl.multiple_of(pair * 128, 128), 128)
        keys = k1[:, columns]
        values = jnp.concatenate([v1[:, columns], jnp.ones((cell_count, 128), BF16)], axis=1)

        def scores(start, half):
            rows = q1[start : start + block, columns]
            return dot_t(jnp.where(lane // 64 == half, rows, BF16(0)), keys)

        def weigh(score):
            top = jnp.max(score, axis=1, keepdims=True)
            return jnp.exp2((score - top) * scale).astype(BF16), top

        def read(weight, top, start, half):
            summed = dot(weight, values)
            return summed[:, :128] / summed[:, 128:], top * scale + jnp.log2(summed[:, 128:])

        items = [(start, half) for start in range(0, count, block) for half in range(2)]
        out = pipelined(items, scores, weigh, read)
        for start in range(0, count, block):
            (first, first_log), (second, second_log) = out[(start, 0)], out[(start, 1)]
            part[pair, start : start + block, :] = jnp.where(lane < 64, first, second).astype(BF16)
            logs = jnp.where(lane < 64, first_log, second_log)
            for begin in range(0, block, slice_rows):
                turned = jnp.transpose(logs[begin : begin + slice_rows, :])
                stat[pair, (start + begin) // slice_rows] = jnp.where(level < 4, turned[0:8], turned[64:72])

    def send_first(pair):
        def send(step, carry):
            place = lax.rem(near + step, inner)
            rows = pl.ds(pl.multiple_of(place * slice_rows, slice_rows), slice_rows)
            pltpu.make_async_remote_copy(
                src_ref=part.at[pair, rows], dst_ref=part_in.at[pair, step],
                send_sem=send_part.at[pair], recv_sem=recv_part.at[pair],
                device_id=near_device(step), device_id_type=MESH,
            ).start()
            pltpu.make_async_remote_copy(
                src_ref=stat.at[pair, place], dst_ref=stat_in.at[pair, step],
                send_sem=send_stat.at[pair], recv_sem=recv_stat.at[pair],
                device_id=near_device(step), device_id_type=MESH,
            ).start()
            return carry

        lax.fori_loop(1, inner, send, 0)

    def wait_for(ref, semaphore):
        pltpu.make_async_copy(ref, ref, semaphore).wait()

    def merge_first(pair):
        wait_for(part_in.at[pair, 1:inner], recv_part.at[pair])
        wait_for(stat_in.at[pair, 1:inner], recv_stat.at[pair])
        rows = pl.ds(pl.multiple_of(near * slice_rows, slice_rows), slice_rows)
        stats = [stat[pair, near]] + [stat_in[pair, step] for step in range(1, inner)]
        turned = jnp.transpose(jnp.concatenate(stats + [jnp.zeros((128 - 8 * inner, 128), F32)], axis=0))
        logs = [
            jnp.where(lane < 64, turned[:, 8 * step : 8 * step + 1], turned[:, 8 * step + 4 : 8 * step + 5])
            for step in range(inner)
        ]
        top = functools.reduce(jnp.maximum, logs)
        summed, total = 0.0, 0.0
        for step in range(inner):
            weight = jnp.exp2(logs[step] - top)
            source = part[pair, rows, :] if step == 0 else part_in[pair, step]
            summed = summed + weight * source.astype(F32)
            total = total + weight
        group[pair, :, :own_rows, :] = (summed / total).reshape(outer, own_rows, 128)
        group[pair, :, own_rows:, :] = (top + jnp.log2(total)).reshape(outer, own_rows, 128)

        def send(step, carry):
            place = lax.rem(far + step, outer)
            pltpu.make_async_remote_copy(
                src_ref=group.at[pair, place], dst_ref=group_in.at[pair, step],
                send_sem=send_group.at[pair], recv_sem=recv_group.at[pair],
                device_id=far_device(step), device_id_type=MESH,
            ).start()
            return carry

        lax.fori_loop(1, outer, send, 0)

    def merge_second(pair):
        wait_for(group_in.at[pair, 1:outer], recv_group.at[pair])
        blocks = [group[pair, far]] + [group_in[pair, step] for step in range(1, outer)]
        logs = [piece[own_rows:] for piece in blocks]
        top = functools.reduce(jnp.maximum, logs)
        summed, total = 0.0, 0.0
        for step in range(outer):
            weight = jnp.exp2(logs[step] - top)
            summed = summed + weight * blocks[step][:own_rows]
            total = total + weight
        own[pair, far] = summed / total

        def send(step, carry):
            pltpu.make_async_remote_copy(
                src_ref=own.at[pair, far], dst_ref=own.at[pair, far],
                send_sem=send_own.at[pair], recv_sem=recv_own.at[pair],
                device_id=far_device(step), device_id_type=MESH,
            ).start()
            return carry

        lax.fori_loop(1, outer, send, 0)

    def spread(pair):
        wait_for(own.at[pair, 1:outer], recv_own.at[pair])
        gathered[pair, near] = own[pair].reshape(slice_rows, 128).astype(BF16)

        def send(step, carry):
            pltpu.make_async_remote_copy(
                src_ref=gathered.at[pair, near], dst_ref=gathered.at[pair, near],
                send_sem=send_read.at[pair], recv_sem=recv_read.at[pair],
                device_id=near_device(step), device_id_type=MESH,
            ).start()
            return carry

        lax.fori_loop(1, inner, send, 0)

    def turn(step, carry):
        @pl.when(step < pairs)
        def _():
            attend(step)

        @pl.when(step == 0)
        def _():
            pl.semaphore_wait(barrier, inner + outer - 2)

        @pl.when(step < pairs)
        def _():
            send_first(step)

        @pl.when(jnp.logical_and(step >= 1, step < pairs + 1))
        def _():
            merge_first(step - 1)

        @pl.when(jnp.logical_and(step >= 2, step < pairs + 2))
        def _():
            merge_second(step - 2)

        @pl.when(step >= 3)
        def _():
            spread(step - 3)

        return carry

    lax.fori_loop(0, pairs + 3, turn, 0)

    for pair in range(pairs):
        wait_for(gathered.at[pair, 1:inner], recv_read.at[pair])
        wide_read[:, pair * 128 : pair * 128 + 128] = gathered[pair].reshape(count, 128)
    state = (latents[...].astype(F32) + dot(wide_read[...], w_o1[...])).astype(BF16)
    k2[...] = dot(state, w_k2[...]).astype(BF16)
    v2[...] = dot(state, w_v2[...]).astype(BF16)
    for pair in range(pairs):
        wait_for(part_in.at[pair, 1:inner], send_part.at[pair])
        wait_for(stat_in.at[pair, 1:inner], send_stat.at[pair])
        wait_for(group_in.at[pair, 1:outer], send_group.at[pair])
        wait_for(own.at[pair, 1:outer], send_own.at[pair])
        wait_for(gathered.at[pair, 1:inner], send_read.at[pair])


def latent_call(scale, q1, k1, v1, latents, w_o1, w_k2, w_v2):
    count, width = q1.shape
    pairs = width // 128
    inner = 8
    outer = lax.axis_size("wide") // inner * lax.axis_size("narrow")
    slice_rows = count // inner
    own_rows = slice_rows // outer
    rows = jax.ShapeDtypeStruct((count, width), BF16)
    return pl.pallas_call(
        functools.partial(latent_kernel, scale, 256),
        out_shape=(rows, rows),
        in_specs=[vmem()] * 7,
        out_specs=[vmem()] * 2,
        scratch_shapes=[
            pltpu.VMEM((pairs, count, 128), BF16),
            pltpu.VMEM((pairs, inner, 8, 128), F32),
            pltpu.VMEM((pairs, inner, slice_rows, 128), BF16),
            pltpu.VMEM((pairs, inner, 8, 128), F32),
            pltpu.VMEM((pairs, outer, 2 * own_rows, 128), F32),
            pltpu.VMEM((pairs, outer, 2 * own_rows, 128), F32),
            pltpu.VMEM((pairs, outer, own_rows, 128), F32),
            pltpu.VMEM((pairs, inner, slice_rows, 128), BF16),
            pltpu.VMEM((count, width), BF16),
        ]
        + [pltpu.SemaphoreType.DMA((pairs,))] * 10,
        compiler_params=pltpu.CompilerParams(
            collective_id=1, has_side_effects=True, vmem_limit_bytes=56 * 2**20
        ),
        name="latents",
    )(q1, k1, v1, latents, w_o1, w_k2, w_v2)


def cell_kernel(scale, q2, k2, v2, cells, w_o2, out):
    count = k2.shape[0]
    heads = q2.shape[1] // 64
    lane = lax.broadcasted_iota(jnp.int32, (1, 128), 1)
    ones = jnp.ones((count, 128), BF16)

    def columns(head):
        return slice(head // 2 * 128, head // 2 * 128 + 128)

    def scores(head):
        return dot_t(jnp.where(lane // 64 == head % 2, q2[:, columns(head)], BF16(0)), k2[:, columns(head)])

    def weigh(score):
        top = jnp.max(score, axis=1, keepdims=True)
        return jnp.exp2((score - top) * scale).astype(BF16), None

    def read(weight, top, head):
        summed = dot(weight, jnp.concatenate([v2[:, columns(head)], ones], axis=1))
        return summed[:, :128] / summed[:, 128:]

    found = pipelined([(head,) for head in range(heads)], scores, weigh, read)
    reads = [
        jnp.where(lane < 64, found[(head,)], found[(head + 1,)]).astype(BF16) for head in range(0, heads, 2)
    ]
    out[...] = cells[...].astype(F32) + dot(jnp.concatenate(reads, axis=1), w_o2[...])


def cell_call(scale, q2, k2, v2, cells, w_o2):
    count, width = q2.shape
    block = 512
    by_rows = pl.BlockSpec((block, width), lambda step: (step, 0))

    def whole(array):
        return pl.BlockSpec(array.shape, lambda step: (0, 0))

    return pl.pallas_call(
        functools.partial(cell_kernel, scale),
        out_shape=jax.ShapeDtypeStruct((count, width), F32),
        grid=(count // block,),
        in_specs=[by_rows, whole(k2), whole(v2), by_rows, whole(w_o2)],
        out_specs=by_rows,
        compiler_params=pltpu.CompilerParams(vmem_limit_bytes=56 * 2**20),
        name="cells",
    )(q2, k2, v2, cells, w_o2)


def per_device(
    flow_field, fluid_mask, conv_weight, latents,
    w_query1, w_key1, w_value1, w_out1, w_query2, w_key2, w_value2, w_out2,
):
    size_x, size_y, size_z, width = flow_field.shape
    scale = 1.8 / math.sqrt(width // HEADS) * math.log2(math.e)
    masked = flow_field * fluid_mask[:, :, :, None].astype(BF16)
    q1, k1, v1, q2 = stencil_call(masked, conv_weight, latents, w_query1, w_key1, w_value1, w_query2)
    k2, v2 = latent_call(scale, q1, k1, v1, latents, w_out1, w_key2, w_value2)
    flat = masked.reshape(size_x * size_y * size_z, width)
    result = cell_call(scale, q2, k2, v2, flat, w_out2)
    return result.reshape(size_x, size_y, size_z, width)


def solution(mesh):
    cells = P("wide", "narrow", None, None)
    return jax.shard_map(
        per_device,
        mesh=mesh,
        in_specs=(cells, P("wide", "narrow", None)) + (P(),) * 10,
        out_specs=cells,
        check_vma=False,
    )
```

time: 489 us -> 114 us (0.23); the launches traced: 484 us -> 114 us
  matrix products: 159 us -> 0 us
  blocking collectives: 132 us -> 0 us
  Pallas kernels: 0 us -> 109 us
  waiting for transfers between devices: 81.6 us -> 0 us
  other arithmetic: 77.7 us -> 4.12 us
  between operations: 14.3 us -> 0.02 us
  starting transfers between devices: 11 us -> 0 us
  local copies, waits for them, and re-layouts: 8.31 us -> 0 us
    dot_general x40 -> x0, matrix products: 159 us -> none  [the longest x16 62.9 us: pair_scores(): lax.dot_general(queries, key_rows, (((1,), (1,)), ((), ())), preferred_el...]
    pallas_call x0 -> x3, Pallas kernels: none -> 109 us  [the longest x1 53.2 us: latent_call(): pl.pallas_call(functools.partial(latent_kernel, scale, 256), out_shape=(r...]
    psum x1 -> x0, waiting for transfers between devices: 72 us -> none  [per_device(): summed, totals = lax.psum((summed1, totals1), ('wide', 'narrow'))]
    pmax x1 -> x0, blocking collectives: 68.1 us -> none  [per_device(): lax.pmax(local_top.astype(jnp.bfloat16), ('wide', 'narrow'))]
    psum x1 -> x0, blocking collectives: 63.9 us -> none  [per_device(): summed, totals = lax.psum((summed1, totals1), ('wide', 'narrow'))]
    reduce_sum x16 -> x0, other arithmetic: 53.1 us -> none  [the longest x8 28.3 us: per_device(): totals = jnp.sum(weights, axis=1, keepdims=True)]
    convert_element_type x3 -> x1, other arithmetic: 18.9 us -> 0.85 us  [per_device(): masked = flow_field * fluid_mask[:, :, :, None].astype(BF16)]
    ppermute x4 -> x0, starting transfers between devices: 10.9 us -> none  [the longest x2 7.72 us: padded_2(): lax.ppermute(tail, axis, [(i, (i + 1) % count) for i in range(ends)])]
  transfers between devices with their start and end apart: 5 -> 0, of which waited for: 5 -> 0; matrix products, arithmetic and copies ran while one was open for 3% -> 0% of each run, Pallas kernels for 0% -> 0%
where the time goes in v1:
time: 114 us
  Pallas kernels  109 us (96%)
  other arithmetic  4.12 us (4%)
    pallas_call x1, Pallas kernels, latent_call(): pl.pallas_call(functools.partial(latent_kernel, scale, 256), out_shape=(r...  53.2 us
    pallas_call x1, Pallas kernels, stencil_call(): pl.pallas_call(stencil_kernel, out_shape=(jax.ShapeDtypeStruct(latents.sh...  31.1 us
    pallas_call x1, Pallas kernels, cell_call(): pl.pallas_call(functools.partial(cell_kernel, scale), out_shape=jax.Shape...  25.2 us
    mul x1, other arithmetic, per_device(): masked = flow_field * fluid_mask[:, :, :, None].astype(BF16)  3.27 us

profile of v1, /device:TPU:1, one launch (start us, length us, event | category | flops | bytes accessed | tf_op | source)
XLA Modules:
  0.0 113.6 jit_solution(6173872258233738940)
XLA Ops:
  0.0 0.8 convert_element_type.4
  0.8 3.3 %broadcast_multiply_fusion.cells = bf16[8,16,16,512]{3,2,1,0:T(8,128)(2,1)} fusion(bf16[8,16,16,512]{3,2,1,0:T(8,128)(2,1)} %param.12, bf16[8,16,16]{2,1,0:T(8,128)(2,1)S(1)} %convert_element_type.4), kind=kLoop, calls=%fused_computation | loop fusion | flops 1048576 | bytes 4198400 | tf_op jit(solution)/shard_map/mul | solution.py:437
  4.1 31.1 %stencil.1 = (bf16[1024,512]{1,0:T(8,128)(2,1)}, bf16[2048,512]{1,0:T(8,128)(2,1)}, bf16[2048,512]{1,0:T(8,128)(2,1)}, bf16[2048,512]{1,0:T(8,128)(2,1)}) custom-call(bf16[8,16,16,512]{3,2,1,0:T(8,128)(2,1)} %broadcast_multiply_fusion.cells, f32[27,512]{1,0:T(8,128)} %conv.1, bf16[1024,512]{1,0:T(8,128)(2,1)} %latents.5, bf16[512,512]{1,0:T(8,128)(2,1)} %w_q1.1, ...), custom_call_target="tpu_custom_call" | custom-call | tf_op jit(solution)/shard_map/stencil/pallas_call | solution.py:119
  35.2 53.2 %latents.4 = (bf16[1024,512]{1,0:T(8,128)(2,1)}, bf16[1024,512]{1,0:T(8,128)(2,1)}) custom-call(bf16[1024,512]{1,0:T(8,128)(2,1)} %get-tuple-element.12.q1, bf16[2048,512]{1,0:T(8,128)(2,1)} %get-tuple-element.13.k1, bf16[2048,512]{1,0:T(8,128)(2,1)} %get-tuple-element.14.v1, bf16[1024,512]{1,0:T(8,128)(2,1)} %latents.5, bf16[512,512]{1,0:T(8,128)(2,1)} %w_o1.1, ...), custom_call_target="tpu_custom_call" | custom-call | tf_op jit(solution)/shard_map/latents/pallas_call | solution.py:361
  88.4 25.2 %cells.1 = f32[2048,512]{1,0:T(8,128)} custom-call(bf16[2048,512]{1,0:T(8,128)(2,1)} %get-tuple-element.11.q2, bf16[1024,512]{1,0:T(8,128)(2,1)} %get-tuple-element.15.k2, bf16[1024,512]{1,0:T(8,128)(2,1)} %get-tuple-element.16.v2, bf16[2048,512]{1,0:T(8,128)(2,1)} %bitcast.2, bf16[512,512]{1,0:T(8,128)(2,1)} %w_o2.1), custom_call_target="tpu_custom_call" | custom-call | tf_op jit(solution)/shard_map/cells/pallas_call | solution.py:420

commit v2 on v1

v2 whole, which is shorter than its diff:
```python
import functools
import math

import jax
import jax.numpy as jnp
from jax import lax
from jax.experimental import pallas as pl
from jax.experimental.pallas import tpu as pltpu
from jax.sharding import PartitionSpec as P

HEADS = 8
MESH = pl.DeviceIdType.MESH
F32 = jnp.float32
BF16 = jnp.bfloat16


def dot(a, b):
    return jnp.dot(a, b, preferred_element_type=F32)


def dot_t(a, b):
    return lax.dot_general(a, b, (((1,), (1,)), ((), ())), preferred_element_type=F32)


def mask_rows(plane):
    size_y, size_z = plane.shape
    row = lax.broadcasted_iota(jnp.int32, (size_y * size_z, size_y), 0)
    column = lax.broadcasted_iota(jnp.int32, (size_y * size_z, size_y), 1)
    spread = dot((row // size_z == column).astype(F32).astype(BF16), plane.astype(F32).astype(BF16))
    row = lax.broadcasted_iota(jnp.int32, (size_y * size_z, size_z), 0)
    column = lax.broadcasted_iota(jnp.int32, (size_y * size_z, size_z), 1)
    picked = jnp.where(row % size_z == column, spread, 0.0).astype(BF16)
    return dot(picked, jnp.ones((size_z, 128), BF16)).astype(BF16)


def vmem():
    return pl.BlockSpec(memory_space=pltpu.VMEM)


def pipelined(items, scores, weigh, read):
    score, weight, top, out = scores(*items[0]), None, None, {}
    for j in range(len(items) + 1):
        later = scores(*items[j + 1]) if j + 1 < len(items) else None
        fresh = weigh(score) if j < len(items) else (None, None)
        if j > 0:
            out[items[j - 1]] = read(weight, top, *items[j - 1])
        score, (weight, top) = later, fresh
    return out


def layer_kernel(
    scale, chunks,
    cells, mask, conv, latents, w_q1, w_k1, w_v1, w_o1, w_q2, w_k2, w_v2,
    out,
    masked, x_side, y_side, corner, pad, taps, mixed, q1, k1, v1, q2,
    part, stat, part_in, stat_in, group, group_in, own, gathered, sums, tops,
    send_side, recv_side,
    send_part, recv_part, send_stat, recv_stat, send_group, recv_group,
    send_own, recv_own, send_read, recv_read,
):
    size_x, size_y, size_z, width = cells.shape
    plane_cells = size_y * size_z
    cell_count = size_x * plane_cells
    block = latents.shape[0] // chunks
    pairs = width // 128
    wide, narrow = lax.axis_index("wide"), lax.axis_index("narrow")
    wides, narrows = lax.axis_size("wide"), lax.axis_size("narrow")
    inner = 8
    outer = wides // inner * narrows
    slice_rows = block * pairs // inner
    own_rows = slice_rows // outer
    floor = wide // inner
    near = wide - floor * inner
    far = floor * narrows + narrow

    def near_device(step):
        return (floor * inner + lax.rem(near + step, inner), narrow)

    def far_device(step):
        place = lax.rem(far + step, outer)
        return ((place // narrows) * inner + near, lax.rem(place, narrows))

    def beside(step_x, step_y):
        return (lax.rem(wide + step_x + wides, wides), lax.rem(narrow + step_y + narrows, narrows))

    barrier = pltpu.get_barrier_semaphore()
    steps = [(1, 0), (-1, 0), (0, 1), (0, -1), (1, 1), (1, -1), (-1, 1), (-1, -1)]

    def greet_near(step, carry):
        pl.semaphore_signal(barrier, inc=1, device_id=near_device(step), device_id_type=MESH)
        return carry

    def greet_far(step, carry):
        pl.semaphore_signal(barrier, inc=1, device_id=far_device(step), device_id_type=MESH)
        return carry

    for step in steps:
        pl.semaphore_signal(barrier, inc=1, device_id=beside(*step), device_id_type=MESH)
    lax.fori_loop(1, outer, greet_far, 0)
    lax.fori_loop(1, inner, greet_near, 0)

    lane = lax.broadcasted_iota(jnp.int32, (1, 128), 1)
    level = lax.broadcasted_iota(jnp.int32, (8, 128), 0)

    def columns(pair):
        return slice(pair * 128, pair * 128 + 128)

    def cover(x, carry):
        fluid = jnp.concatenate([mask_rows(mask[x])] * pairs, axis=1)
        plane = (cells[x].reshape(plane_cells, width) * fluid).reshape(size_y, size_z, width)
        masked[x] = plane
        pad[x + 1, 1 : size_y + 1] = plane.astype(F32)
        return carry

    lax.fori_loop(0, size_x, cover, 0)
    for tap in range(27):
        taps[tap] = jnp.broadcast_to(conv[tap : tap + 1, :], (8, width))

    pl.semaphore_wait(barrier, inner + outer - 2 + len(steps))
    copies = []
    for index, (step_x, step_y) in enumerate(steps):
        from_x = size_x - 1 if step_x == 1 else 0
        from_y = size_y - 1 if step_y == 1 else 0
        low_x = 0 if step_x == 1 else 1
        low_y = 0 if step_y == 1 else 1
        if step_y == 0:
            source, target = masked.at[from_x], x_side.at[low_x]
        elif step_x == 0:
            source, target = masked.at[:, from_y], y_side.at[low_y]
        else:
            source, target = masked.at[from_x, from_y], corner.at[low_x, low_y]
        copy = pltpu.make_async_remote_copy(
            src_ref=source, dst_ref=target, send_sem=send_side.at[index], recv_sem=recv_side.at[index],
            device_id=beside(step_x, step_y), device_id_type=MESH,
        )
        copy.start()
        copies.append(copy)

    depth = lax.broadcasted_iota(jnp.int32, (size_z, 128), 0)

    def strip(x, column, first, last):
        lanes = columns(column)
        found = {}
        centre = {}
        for y in range(first - 1, last + 1):
            for a in range(3):
                value = pad[x + a, y + 1, :, lanes].reshape(size_z // 8, 8, 128)
                for b in range(3):
                    target = y + 1 - b
                    if not first <= target < last:
                        continue
                    if a == 1 and b == 1:
                        centre[target] = value
                    for c in range(3):
                        term = value * taps[9 * a + 3 * b + c, :, lanes]
                        key = (target, c)
                        found[key] = found[key] + term if key in found else term
            target = y - 1
            if first <= target < last:
                low, mid, high = [found.pop((target, c)).reshape(size_z, 128) for c in range(3)]
                below = jnp.where(depth == 0, 0.0, pltpu.roll(low, 1, 0))
                above = jnp.where(depth == size_z - 1, 0.0, pltpu.roll(high, size_z - 1, 0))
                total = (centre.pop(target).reshape(size_z, 128) + mid) + (below + above)
                start = pl.multiple_of((x * size_y + target) * size_z, size_z)
                mixed[pl.ds(start, size_z), lanes] = total.astype(BF16)

    def middle(x, carry):
        for column in range(pairs):
            strip(x, column, 1, size_y - 1)
        return carry

    lax.fori_loop(1, size_x - 1, middle, 0)
    q1[...] = dot(latents[...], w_q1[...]).astype(BF16)

    for copy in copies:
        copy.wait()
    for low in range(2):
        keep_x = (wide > 0) if low == 0 else (wide < wides - 1)
        keep_y = (narrow > 0) if low == 0 else (narrow < narrows - 1)
        pad[low * (size_x + 1), 1 : size_y + 1] = jnp.where(keep_x, x_side[low].astype(F32), 0.0)
        pad[1 : size_x + 1, low * (size_y + 1)] = jnp.where(keep_y, y_side[low].astype(F32), 0.0)
        for low_y in range(2):
            keep = jnp.logical_and(keep_x, (narrow > 0) if low_y == 0 else (narrow < narrows - 1))
            pad[low * (size_x + 1), low_y * (size_y + 1)] = jnp.where(keep, corner[low, low_y].astype(F32), 0.0)

    def ends(side, carry):
        for column in range(pairs):
            strip(side * (size_x - 1), column, 0, size_y)
        return carry

    def edges(x, carry):
        for column in range(pairs):
            strip(x, column, 0, 1)
            strip(x, column, size_y - 1, size_y)
        return carry

    lax.fori_loop(0, 2, ends, 0)
    lax.fori_loop(1, size_x - 1, edges, 0)

    tall = cell_count // 4

    def project_first(step, carry):
        rows = pl.ds(pl.multiple_of(step * tall, tall), tall)
        k1[rows, :] = dot(mixed[rows, :], w_k1[...]).astype(BF16)
        v1[rows, :] = dot(mixed[rows, :], w_v1[...]).astype(BF16)
        return carry

    def project_second(step, carry):
        rows = pl.ds(pl.multiple_of(step * tall, tall), tall)
        q2[rows, :] = dot(mixed[rows, :], w_q2[...]).astype(BF16)
        return carry

    lax.fori_loop(0, 4, project_first, 0)

    def attend(chunk):
        rows = pl.ds(pl.multiple_of(chunk * block, block), block)

        def scores(pair, half):
            return dot_t(jnp.where(lane // 64 == half, q1[rows, columns(pair)], BF16(0)), k1[:, columns(pair)])

        def weigh(score):
            top = jnp.max(score, axis=1, keepdims=True)
            return jnp.exp2((score - top) * scale).astype(BF16), top

        def read(weight, top, pair, half):
            values = jnp.concatenate([v1[:, columns(pair)], jnp.ones((cell_count, 128), BF16)], axis=1)
            summed = dot(weight, values)
            return summed[:, :128] / summed[:, 128:], top * scale + jnp.log2(summed[:, 128:])

        items = [(pair, half) for pair in range(pairs) for half in range(2)]
        found = pipelined(items, scores, weigh, read)
        for pair in range(pairs):
            (first, first_log), (second, second_log) = found[(pair, 0)], found[(pair, 1)]
            start = pair * block
            part[chunk, start : start + block, :] = jnp.where(lane < 64, first, second).astype(BF16)
            logs = jnp.where(lane < 64, first_log, second_log)
            for begin in range(0, block, slice_rows):
                turned = jnp.transpose(logs[begin : begin + slice_rows, :])
                stat[chunk, (start + begin) // slice_rows] = jnp.where(level < 4, turned[0:8], turned[64:72])

    def send_first(chunk):
        def send(step, carry):
            place = lax.rem(near + step, inner)
            rows = pl.ds(pl.multiple_of(place * slice_rows, slice_rows), slice_rows)
            pltpu.make_async_remote_copy(
                src_ref=part.at[chunk, rows], dst_ref=part_in.at[chunk, step],
                send_sem=send_part.at[chunk], recv_sem=recv_part.at[chunk],
                device_id=near_device(step), device_id_type=MESH,
            ).start()
            pltpu.make_async_remote_copy(
                src_ref=stat.at[chunk, place], dst_ref=stat_in.at[chunk, step],
                send_sem=send_stat.at[chunk], recv_sem=recv_stat.at[chunk],
                device_id=near_device(step), device_id_type=MESH,
            ).start()
            return carry

        lax.fori_loop(1, inner, send, 0)

    def wait_for(ref, semaphore):
        pltpu.make_async_copy(ref, ref, semaphore).wait()

    def merge_first(chunk):
        wait_for(part_in.at[chunk, 1:inner], recv_part.at[chunk])
        wait_for(stat_in.at[chunk, 1:inner], recv_stat.at[chunk])
        rows = pl.ds(pl.multiple_of(near * slice_rows, slice_rows), slice_rows)
        stats = [stat[chunk, near]] + [stat_in[chunk, step] for step in range(1, inner)]
        turned = jnp.transpose(jnp.concatenate(stats + [jnp.zeros((128 - 8 * inner, 128), F32)], axis=0))
        logs = [
            jnp.where(lane < 64, turned[:, 8 * step : 8 * step + 1], turned[:, 8 * step + 4 : 8 * step + 5])
            for step in range(inner)
        ]
        top = functools.reduce(jnp.maximum, logs)
        summed, total = 0.0, 0.0
        for step in range(inner):
            weight = jnp.exp2(logs[step] - top)
            source = part[chunk, rows, :] if step == 0 else part_in[chunk, step]
            summed = summed + weight * source.astype(F32)
            total = total + weight
        group[chunk, :, :own_rows, :] = (summed / total).reshape(outer, own_rows, 128)
        group[chunk, :, own_rows:, :] = (top + jnp.log2(total)).reshape(outer, own_rows, 128)

        def send(step, carry):
            place = lax.rem(far + step, outer)
            pltpu.make_async_remote_copy(
                src_ref=group.at[chunk, place], dst_ref=group_in.at[chunk, step],
                send_sem=send_group.at[chunk], recv_sem=recv_group.at[chunk],
                device_id=far_device(step), device_id_type=MESH,
            ).start()
            return carry

        lax.fori_loop(1, outer, send, 0)

    def merge_second(chunk):
        wait_for(group_in.at[chunk, 1:outer], recv_group.at[chunk])
        blocks = [group[chunk, far]] + [group_in[chunk, step] for step in range(1, outer)]
        logs = [piece[own_rows:] for piece in blocks]
        top = functools.reduce(jnp.maximum, logs)
        summed, total = 0.0, 0.0
        for step in range(outer):
            weight = jnp.exp2(logs[step] - top)
            summed = summed + weight * blocks[step][:own_rows]
            total = total + weight
        own[chunk, far] = summed / total

        def send(step, carry):
            pltpu.make_async_remote_copy(
                src_ref=own.at[chunk, far], dst_ref=own.at[chunk, far],
                send_sem=send_own.at[chunk], recv_sem=recv_own.at[chunk],
                device_id=far_device(step), device_id_type=MESH,
            ).start()
            return carry

        lax.fori_loop(1, outer, send, 0)

    def spread(chunk):
        wait_for(own.at[chunk, 1:outer], recv_own.at[chunk])
        gathered[chunk, near] = own[chunk].reshape(slice_rows, 128).astype(BF16)

        def send(step, carry):
            pltpu.make_async_remote_copy(
                src_ref=gathered.at[chunk, near], dst_ref=gathered.at[chunk, near],
                send_sem=send_read.at[chunk], recv_sem=recv_read.at[chunk],
                device_id=near_device(step), device_id_type=MESH,
            ).start()
            return carry

        lax.fori_loop(1, inner, send, 0)

    def turn(step, carry):
        attend(step)
        send_first(step)

        @pl.when(step >= 3)
        def _():
            spread(step - 3)

        @pl.when(step >= 2)
        def _():
            merge_second(step - 2)

        @pl.when(step >= 1)
        def _():
            merge_first(step - 1)

        return carry

    lax.fori_loop(0, chunks, turn, 0)

    def latent_side(chunk):
        wait_for(gathered.at[chunk, 1:inner], recv_read.at[chunk])
        every = gathered[chunk].reshape(pairs, block, 128)
        read1 = jnp.concatenate([every[pair] for pair in range(pairs)], axis=1)
        rows = slice(chunk * block, chunk * block + block)
        state = (latents[rows, :].astype(F32) + dot(read1, w_o1[...])).astype(BF16)
        return dot(state, w_k2[...]).astype(BF16), dot(state, w_v2[...]).astype(BF16)

    high = cell_count // 2

    def absorb(part_index, keys, values, between):
        last = part_index == 1
        span = keys.shape[0]

        def rows_of(step, carry):
            rows = pl.ds(pl.multiple_of(step * high, high), high)

            def scores(pair, half):
                return dot_t(jnp.where(lane // 64 == half, q2[rows, columns(pair)], BF16(0)), keys[:, columns(pair)])

            def update(score, pair, half):
                top = jnp.max(score, axis=1, keepdims=True)
                shrink = None
                if last:
                    before = tops[2 * pair + half, rows, :]
                    top = jnp.maximum(before, top)
                    shrink = jnp.exp2((before - top) * scale)
                    top = jnp.concatenate([top] * (span // 128), axis=1)
                else:
                    tops[2 * pair + half, rows, :] = jnp.broadcast_to(top, (high, 128))
                return jnp.exp2((score - top) * scale).astype(BF16), shrink

            def add(weight, shrink, pair, half):
                both = jnp.where(lane // 64 == half, values[:, columns(pair)], BF16(1))
                summed = dot(weight, both)
                if not last:
                    sums[2 * pair + half, rows, :] = summed
                    return None
                summed = summed + shrink * sums[2 * pair + half, rows, :]
                return summed / pltpu.roll(summed, 64, 1)

            items = [(pair, half) for pair in range(pairs) for half in range(2)]
            score, weight, shrink, found = scores(*items[0]), None, None, {}
            for j in range(len(items) + 1):
                later = scores(*items[j + 1]) if j + 1 < len(items) else None
                new = update(score, *items[j]) if j < len(items) else (None, None)
                if j > 0:
                    found[items[j - 1]] = add(weight, shrink, *items[j - 1])
                    if last and items[j - 1][1] == 1:
                        pair = items[j - 1][0]
                        joined = jnp.where(lane < 64, found[(pair, 0)], found[(pair, 1)])
                        out[rows, columns(pair)] = joined.astype(BF16)
                score, (weight, shrink) = later, new
            if between is not None:

                @pl.when(step == 0)
                def _():
                    between()

            return carry

        lax.fori_loop(0, 2, rows_of, 0)

    lax.fori_loop(0, 4, project_second, 0)
    spread(chunks - 3)
    merge_second(chunks - 2)
    merge_first(chunks - 1)
    early = [latent_side(0)]
    spread(chunks - 2)
    early.append(latent_side(1))
    merge_second(chunks - 1)
    absorb(
        0,
        jnp.concatenate([keys for keys, _ in early], axis=0),
        jnp.concatenate([values for _, values in early], axis=0),
        lambda: spread(chunks - 1),
    )
    late = [latent_side(2), latent_side(3)]
    absorb(
        1,
        jnp.concatenate([keys for keys, _ in late], axis=0),
        jnp.concatenate([values for _, values in late], axis=0),
        None,
    )
    for chunk in range(chunks):
        wait_for(part_in.at[chunk, 1:inner], send_part.at[chunk])
        wait_for(stat_in.at[chunk, 1:inner], send_stat.at[chunk])
        wait_for(group_in.at[chunk, 1:outer], send_group.at[chunk])
        wait_for(own.at[chunk, 1:outer], send_own.at[chunk])
        wait_for(gathered.at[chunk, 1:inner], send_read.at[chunk])


def layer_call(scale, cells, mask, conv, latents, *weights):
    chunks = 4
    size_x, size_y, size_z, width = cells.shape
    count = size_x * size_y * size_z
    rows = latents.shape[0] // chunks * (width // 128)
    inner = 8
    outer = lax.axis_size("wide") // inner * lax.axis_size("narrow")
    slice_rows = rows // inner
    own_rows = slice_rows // outer
    return pl.pallas_call(
        functools.partial(layer_kernel, scale, chunks),
        out_shape=jax.ShapeDtypeStruct((count, width), BF16),
        in_specs=[vmem()] * 11,
        out_specs=vmem(),
        scratch_shapes=[
            pltpu.VMEM(cells.shape, BF16),
            pltpu.VMEM((2, size_y, size_z, width), BF16),
            pltpu.VMEM((2, size_x, size_z, width), BF16),
            pltpu.VMEM((2, 2, size_z, width), BF16),
            pltpu.VMEM((size_x + 2, size_y + 2, size_z, width), F32),
            pltpu.VMEM((27, 8, width), F32),
            pltpu.VMEM((count, width), BF16),
            pltpu.VMEM(latents.shape, BF16),
            pltpu.VMEM((count, width), BF16),
            pltpu.VMEM((count, width), BF16),
            pltpu.VMEM((count, width), BF16),
            pltpu.VMEM((chunks, rows, 128), BF16),
            pltpu.VMEM((chunks, inner, 8, 128), F32),
            pltpu.VMEM((chunks, inner, slice_rows, 128), BF16),
            pltpu.VMEM((chunks, inner, 8, 128), F32),
            pltpu.VMEM((chunks, outer, 2 * own_rows, 128), F32),
            pltpu.VMEM((chunks, outer, 2 * own_rows, 128), F32),
            pltpu.VMEM((chunks, outer, own_rows, 128), F32),
            pltpu.VMEM((chunks, inner, slice_rows, 128), BF16),
            pltpu.VMEM((width // 64, count, 128), F32),
            pltpu.VMEM((width // 64, count, 128), F32),
        ]
        + [pltpu.SemaphoreType.DMA((8,))] * 2
        + [pltpu.SemaphoreType.DMA((chunks,))] * 10,
        compiler_params=pltpu.CompilerParams(
            collective_id=0, has_side_effects=True, vmem_limit_bytes=62 * 2**20
        ),
        name="layer",
    )(cells, mask, conv, latents, *weights)


def project_kernel(read2, cells, mask, w_o2, out):
    width = read2.shape[1]
    planes = mask.shape[0]
    fluid = jnp.concatenate([mask_rows(mask[x]) for x in range(planes)], axis=0)
    masked = cells[...] * jnp.concatenate([fluid] * (width // 128), axis=1)
    out[...] = masked.astype(F32) + dot(read2[...], w_o2[...])


def project_call(read2, cells, mask, w_o2):
    count, width = read2.shape
    size_x, size_y, size_z = mask.shape
    planes = 2
    by_rows = pl.BlockSpec((planes * size_y * size_z, width), lambda step: (step, 0))
    return pl.pallas_call(
        project_kernel,
        out_shape=jax.ShapeDtypeStruct((count, width), F32),
        grid=(size_x // planes,),
        in_specs=[
            by_rows,
            by_rows,
            pl.BlockSpec((planes, size_y, size_z), lambda step: (step, 0, 0)),
            pl.BlockSpec(w_o2.shape, lambda step: (0, 0)),
        ],
        out_specs=by_rows,
        compiler_params=pltpu.CompilerParams(vmem_limit_bytes=32 * 2**20),
        name="project",
    )(read2, cells, mask, w_o2)


def per_device(
    flow_field, fluid_mask, conv_weight, latents,
    w_query1, w_key1, w_value1, w_out1, w_query2, w_key2, w_value2, w_out2,
):
    size_x, size_y, size_z, width = flow_field.shape
    scale = 1.8 / math.sqrt(width // HEADS) * math.log2(math.e)
    read2 = layer_call(
        scale, flow_field, fluid_mask, conv_weight, latents,
        w_query1, w_key1, w_value1, w_out1, w_query2, w_key2, w_value2,
    )
    flat = flow_field.reshape(size_x * size_y * size_z, width)
    return project_call(read2, flat, fluid_mask, w_out2).reshape(size_x, size_y, size_z, width)


def solution(mesh):
    cells = P("wide", "narrow", None, None)
    return jax.shard_map(
        per_device,
        mesh=mesh,
        in_specs=(cells, P("wide", "narrow", None)) + (P(),) * 10,
        out_specs=cells,
        check_vma=False,
    )
```

time: 114 us -> 101 us (0.89)
  Pallas kernels: 109 us -> 97.9 us
  other arithmetic: 4.12 us -> 0 us
  local copies, waits for them, and re-layouts: 0 us -> 3.18 us
    pallas_call x3 -> x2, Pallas kernels: 109 us -> 97.9 us  [the longest x1 94.2 us: layer_call(): pl.pallas_call(functools.partial(layer_kernel, scale, chunks), out_shape=...]
    mul x1 -> x0, other arithmetic: 3.27 us -> none  [per_device(): masked = flow_field * fluid_mask[:, :, :, None].astype(BF16)]
    unnamed x0 -> x8, local copies, waits for them, and re-layouts: none -> 3.18 us
where the time goes in v2:
time: 101 us
  Pallas kernels  97.9 us (97%)
  local copies, waits for them, and re-layouts  3.18 us (3%)
    pallas_call x1, Pallas kernels, layer_call(): pl.pallas_call(functools.partial(layer_kernel, scale, chunks), out_shape=...  94.2 us
    pallas_call x1, Pallas kernels, project_call(): pl.pallas_call(project_kernel, out_shape=jax.ShapeDtypeStruct((count, wid...  3.7 us
    unnamed x8, local copies, waits for them, and re-layouts  3.18 us

profile of v2, /device:TPU:1, one launch (start us, length us, event | category | flops | bytes accessed | tf_op | source)
XLA Modules:
  0.0 101.2 jit_solution(16393563240847512814)
XLA Ops:
  0.0 0.0 copy-start.2
  0.0 0.0 copy-start.3
  0.0 94.2 %layer.1.read2 = bf16[2048,512]{1,0:T(8,128)(2,1)} custom-call(bf16[8,16,16,512]{3,2,1,0:T(8,128)(2,1)} %cells.1, s32[8,16,16]{2,1,0:T(8,128)} %mask.3, f32[27,512]{1,0:T(8,128)} %conv.1, bf16[1024,512]{1,0:T(8,128)(2,1)} %latents.1, bf16[512,512]{1,0:T(8,128)(2,1)} %w_q1.1, bf16[512,512]{1,0:T(8,128)(2,1)} %w_k1.1, bf16[512,512]{1,0:T(8,128)(2,1)} %w_v1.1, ...), custom_call_target="tpu_custom_call" | custom-call | tf_op jit(solution)/shard_map/layer/pallas_call | solution.py:450
  94.3 0.0 copy-done.2
  94.3 0.0 copy-done.3
  94.3 0.0 copy-start
  94.3 1.6 %copy-done = bf16[8,16,16,512]{3,2,1,0:T(8,128)(2,1)S(1)} copy-done((bf16[8,16,16,512]{3,2,1,0:T(8,128)(2,1)S(1)}, bf16[8,16,16,512]{3,2,1,0:T(8,128)(2,1)}, u32[]{:S(2)}) %copy-start) | copy-done | bytes 2097176
  95.9 0.0 copy-start.1
  95.9 1.6 %copy-done.1 = bf16[2048,512]{1,0:T(8,128)(2,1)S(1)} copy-done((bf16[2048,512]{1,0:T(8,128)(2,1)S(1)}, bf16[2048,512]{1,0:T(8,128)(2,1)}, u32[]{:S(2)}) %copy-start.1) | copy-done | bytes 2097176
  97.5 3.7 %project.1 = f32[2048,512]{1,0:T(8,128)} custom-call(bf16[2048,512]{1,0:T(8,128)(2,1)S(1)} %copy-done.1, bf16[2048,512]{1,0:T(8,128)(2,1)S(1)} %bitcast.2, s32[8,16,16]{2,1,0:T(8,128)S(1)} %copy-done.3, bf16[512,512]{1,0:T(8,128)(2,1)S(1)} %copy-done.2), custom_call_target="tpu_custom_call" | custom-call | tf_op jit(solution)/shard_map/project/pallas_call | solution.py:500
Async XLA Ops:
  0.0 94.3 %copy-start.2 = (bf16[512,512]{1,0:T(8,128)(2,1)S(1)}, bf16[512,512]{1,0:T(8,128)(2,1)}, u32[]{:S(2)}) copy-start(bf16[512,512]{1,0:T(8,128)(2,1)} %w_o2.1) | copy-start | bytes 1572868
  0.0 94.3 %copy-start.3 = (s32[8,16,16]{2,1,0:T(8,128)S(1)}, s32[8,16,16]{2,1,0:T(8,128)}, u32[]{:S(2)}) copy-start(s32[8,16,16]{2,1,0:T(8,128)} %mask.3) | copy-start | bytes 24580
  94.3 1.6 %copy-start = (bf16[8,16,16,512]{3,2,1,0:T(8,128)(2,1)S(1)}, bf16[8,16,16,512]{3,2,1,0:T(8,128)(2,1)}, u32[]{:S(2)}) copy-start(bf16[8,16,16,512]{3,2,1,0:T(8,128)(2,1)} %cells.1) | copy-start | bytes 6291460
  95.9 1.6 %copy-start.1 = (bf16[2048,512]{1,0:T(8,128)(2,1)S(1)}, bf16[2048,512]{1,0:T(8,128)(2,1)}, u32[]{:S(2)}) copy-start(bf16[2048,512]{1,0:T(8,128)(2,1)} %layer.1.read2) | copy-start | bytes 6291460

commit v3 on v2

--- a/solution.py
+++ b/solution.py
@@ -50,14 +50,23 @@
 
 def layer_kernel(
     scale, chunks,
-    cells, mask, conv, latents, w_q1, w_k1, w_v1, w_o1, w_q2, w_k2, w_v2,
-    out,
+    cells, mask, conv, *rest,
+):
+    sources, out = rest[:9], rest[9]
+    latents, w_q1, w_k1, w_v1, w_q2, w_o1, w_k2, w_v2, w_o2 = rest[10:19]
+    (
     masked, x_side, y_side, corner, pad, taps, mixed, q1, k1, v1, q2,
-    part, stat, part_in, stat_in, group, group_in, own, gathered, sums, tops,
+    part, stat, part_in, stat_in, group, group_in, own, gathered, sums, tops, staged,
     send_side, recv_side,
     send_part, recv_part, send_stat, recv_stat, send_group, recv_group,
-    send_own, recv_own, send_read, recv_read,
-):
+    send_own, recv_own, send_read, recv_read, load_sem, store_sem,
+    ) = rest[19:]
+    loads = [
+        pltpu.make_async_copy(source, target, load_sem.at[index])
+        for index, (source, target) in enumerate(zip(sources, rest[10:19]))
+    ]
+    for load in loads:
+        load.start()
     size_x, size_y, size_z, width = cells.shape
     plane_cells = size_y * size_z
     cell_count = size_x * plane_cells
@@ -140,29 +149,21 @@
 
     def strip(x, column, first, last):
         lanes = columns(column)
-        found = {}
-        centre = {}
-        for y in range(first - 1, last + 1):
+        for y in range(first, last):
+            found = [None] * 3
             for a in range(3):
-                value = pad[x + a, y + 1, :, lanes].reshape(size_z // 8, 8, 128)
                 for b in range(3):
-                    target = y + 1 - b
-                    if not first <= target < last:
-                        continue
+                    value = pad[x + a, y + b, :, lanes].reshape(size_z // 8, 8, 128)
                     if a == 1 and b == 1:
-                        centre[target] = value
+                        centre = value
                     for c in range(3):
                         term = value * taps[9 * a + 3 * b + c, :, lanes]
-                        key = (target, c)
-                        found[key] = found[key] + term if key in found else term
-            target = y - 1
-            if first <= target < last:
-                low, mid, high = [found.pop((target, c)).reshape(size_z, 128) for c in range(3)]
-                below = jnp.where(depth == 0, 0.0, pltpu.roll(low, 1, 0))
-                above = jnp.where(depth == size_z - 1, 0.0, pltpu.roll(high, size_z - 1, 0))
-                total = (centre.pop(target).reshape(size_z, 128) + mid) + (below + above)
-                start = pl.multiple_of((x * size_y + target) * size_z, size_z)
-                mixed[pl.ds(start, size_z), lanes] = total.astype(BF16)
+                        found[c] = term if found[c] is None else found[c] + term
+            centre, low, mid, high = [piece.reshape(size_z, 128) for piece in [centre] + found]
+            below = jnp.where(depth == 0, 0.0, pltpu.roll(low, 1, 0))
+            above = jnp.where(depth == size_z - 1, 0.0, pltpu.roll(high, size_z - 1, 0))
+            start = pl.multiple_of((x * size_y + y) * size_z, size_z)
+            mixed[pl.ds(start, size_z), lanes] = ((centre + mid) + (below + above)).astype(BF16)
 
     def middle(x, carry):
         for column in range(pairs):
@@ -170,6 +171,8 @@
         return carry
 
     lax.fori_loop(1, size_x - 1, middle, 0)
+    loads[0].wait()
+    loads[1].wait()
     q1[...] = dot(latents[...], w_q1[...]).astype(BF16)
 
     for copy in copies:
@@ -210,6 +213,8 @@
         q2[rows, :] = dot(mixed[rows, :], w_q2[...]).astype(BF16)
         return carry
 
+    for load in loads[2:]:
+        load.wait()
     lax.fori_loop(0, 4, project_first, 0)
 
     def attend(chunk):
@@ -354,11 +359,16 @@
         state = (latents[rows, :].astype(F32) + dot(read1, w_o1[...])).astype(BF16)
         return dot(state, w_k2[...]).astype(BF16), dot(state, w_v2[...]).astype(BF16)
 
-    high = cell_count // 2
+    high = cell_count // 4
+
+    def leave(step):
+        rows = pl.ds(pl.multiple_of(step * high, high), high)
+        return pltpu.make_async_copy(staged.at[step], out.at[rows], store_sem.at[step])
 
     def absorb(part_index, keys, values, between):
         last = part_index == 1
         span = keys.shape[0]
+        per = size_x // 4
 
         def rows_of(step, carry):
             rows = pl.ds(pl.multiple_of(step * high, high), high)
@@ -388,7 +398,7 @@
                 return summed / pltpu.roll(summed, 64, 1)
 
             items = [(pair, half) for pair in range(pairs) for half in range(2)]
-            score, weight, shrink, found = scores(*items[0]), None, None, {}
+            score, weight, shrink, found, joined = scores(*items[0]), None, None, {}, []
             for j in range(len(items) + 1):
                 later = scores(*items[j + 1]) if j + 1 < len(items) else None
                 new = update(score, *items[j]) if j < len(items) else (None, None)
@@ -396,32 +406,39 @@
                     found[items[j - 1]] = add(weight, shrink, *items[j - 1])
                     if last and items[j - 1][1] == 1:
                         pair = items[j - 1][0]
-                        joined = jnp.where(lane < 64, found[(pair, 0)], found[(pair, 1)])
-                        out[rows, columns(pair)] = joined.astype(BF16)
+                        joined.append(jnp.where(lane < 64, found[(pair, 0)], found[(pair, 1)]).astype(BF16))
                 score, (weight, shrink) = later, new
-            if between is not None:
-
-                @pl.when(step == 0)
-                def _():
-                    between()
-
+            if last:
+                residual = masked[pl.ds(step * per, per)].reshape(high, width).astype(F32)
+                staged[step] = residual + dot(jnp.concatenate(joined, axis=1), w_o2[...])
+                leave(step).start()
+            else:
+                between(step)
             return carry
 
-        lax.fori_loop(0, 2, rows_of, 0)
+        lax.fori_loop(0, 4, rows_of, 0)
 
     lax.fori_loop(0, 4, project_second, 0)
     spread(chunks - 3)
     merge_second(chunks - 2)
     merge_first(chunks - 1)
-    early = [latent_side(0)]
-    spread(chunks - 2)
-    early.append(latent_side(1))
-    merge_second(chunks - 1)
+    early = [latent_side(0), latent_side(1)]
+
+    def between(step):
+        @pl.when(step == 0)
+        def _():
+            spread(chunks - 2)
+            merge_second(chunks - 1)
+
+        @pl.when(step == 2)
+        def _():
+            spread(chunks - 1)
+
     absorb(
         0,
         jnp.concatenate([keys for keys, _ in early], axis=0),
         jnp.concatenate([values for _, values in early], axis=0),
-        lambda: spread(chunks - 1),
+        between,
     )
     late = [latent_side(2), latent_side(3)]
     absorb(
@@ -436,6 +453,8 @@
         wait_for(group_in.at[chunk, 1:outer], send_group.at[chunk])
         wait_for(own.at[chunk, 1:outer], send_own.at[chunk])
         wait_for(gathered.at[chunk, 1:inner], send_read.at[chunk])
+    for step in range(4):
+        leave(step).wait()
 
 
 def layer_call(scale, cells, mask, conv, latents, *weights):
@@ -449,10 +468,11 @@
     own_rows = slice_rows // outer
     return pl.pallas_call(
         functools.partial(layer_kernel, scale, chunks),
-        out_shape=jax.ShapeDtypeStruct((count, width), BF16),
-        in_specs=[vmem()] * 11,
-        out_specs=vmem(),
-        scratch_shapes=[
+        out_shape=jax.ShapeDtypeStruct((count, width), F32),
+        in_specs=[vmem()] * 3 + [pl.BlockSpec(memory_space=pl.ANY)] * 9,
+        out_specs=pl.BlockSpec(memory_space=pl.ANY),
+        scratch_shapes=[pltpu.VMEM(array.shape, array.dtype) for array in (latents, *weights)]
+        + [
             pltpu.VMEM(cells.shape, BF16),
             pltpu.VMEM((2, size_y, size_z, width), BF16),
             pltpu.VMEM((2, size_x, size_z, width), BF16),
@@ -474,43 +494,16 @@
             pltpu.VMEM((chunks, inner, slice_rows, 128), BF16),
             pltpu.VMEM((width // 64, count, 128), F32),
             pltpu.VMEM((width // 64, count, 128), F32),
+            pltpu.VMEM((4, count // 4, width), F32),
         ]
         + [pltpu.SemaphoreType.DMA((8,))] * 2
-        + [pltpu.SemaphoreType.DMA((chunks,))] * 10,
+        + [pltpu.SemaphoreType.DMA((chunks,))] * 10
+        + [pltpu.SemaphoreType.DMA((9,)), pltpu.SemaphoreType.DMA((4,))],
         compiler_params=pltpu.CompilerParams(
             collective_id=0, has_side_effects=True, vmem_limit_bytes=62 * 2**20
         ),
         name="layer",
     )(cells, mask, conv, latents, *weights)
-
-
-def project_kernel(read2, cells, mask, w_o2, out):
-    width = read2.shape[1]
-    planes = mask.shape[0]
-    fluid = jnp.concatenate([mask_rows(mask[x]) for x in range(planes)], axis=0)
-    masked = cells[...] * jnp.concatenate([fluid] * (width // 128), axis=1)
-    out[...] = masked.astype(F32) + dot(read2[...], w_o2[...])
-
-
-def project_call(read2, cells, mask, w_o2):
-    count, width = read2.shape
-    size_x, size_y, size_z = mask.shape
-    planes = 2
-    by_rows = pl.BlockSpec((planes * size_y * size_z, width), lambda step: (step, 0))
-    return pl.pallas_call(
-        project_kernel,
-        out_shape=jax.ShapeDtypeStruct((count, width), F32),
-        grid=(size_x // planes,),
-        in_specs=[
-            by_rows,
-            by_rows,
-            pl.BlockSpec((planes, size_y, size_z), lambda step: (step, 0, 0)),
-            pl.BlockSpec(w_o2.shape, lambda step: (0, 0)),
-        ],
-        out_specs=by_rows,
-        compiler_params=pltpu.CompilerParams(vmem_limit_bytes=32 * 2**20),
-        name="project",
-    )(read2, cells, mask, w_o2)
 
 
 def per_device(
@@ -519,12 +512,11 @@
 ):
     size_x, size_y, size_z, width = flow_field.shape
     scale = 1.8 / math.sqrt(width // HEADS) * math.log2(math.e)
-    read2 = layer_call(
+    result = layer_call(
         scale, flow_field, fluid_mask, conv_weight, latents,
-        w_query1, w_key1, w_value1, w_out1, w_query2, w_key2, w_value2,
+        w_query1, w_key1, w_value1, w_query2, w_out1, w_key2, w_value2, w_out2,
     )
-    flat = flow_field.reshape(size_x * size_y * size_z, width)
-    return project_call(read2, flat, fluid_mask, w_out2).reshape(size_x, size_y, size_z, width)
+    return result.reshape(size_x, size_y, size_z, width)
 
 
 def solution(mesh):

time: 101 us -> 91.8 us (0.909)
  Pallas kernels: 97.9 us -> 86.5 us
  local copies, waits for them, and re-layouts: 3.18 us -> 5.04 us
    pallas_call x1, Pallas kernels: 94.2 us -> 86.5 us  [layer_call(): pl.pallas_call(functools.partial(layer_kernel, scale, chunks), out_shape=...]
    pallas_call x1 -> x0, Pallas kernels: 3.7 us -> none  [project_call(): pl.pallas_call(project_kernel, out_shape=jax.ShapeDtypeStruct((count, wid...]
    unnamed x8 -> x1, local copies, waits for them, and re-layouts: 3.18 us -> 5.04 us
where the time goes in v3:
time: 91.8 us; the launch traced here: 91.6 us
  Pallas kernels  86.5 us (94%)
  local copies, waits for them, and re-layouts  5.04 us (5%)
    pallas_call x1, Pallas kernels, layer_call(): pl.pallas_call(functools.partial(layer_kernel, scale, chunks), out_shape=...  86.5 us
    unnamed x1, local copies, waits for them, and re-layouts  5.04 us

profile of v3, /device:TPU:1, one launch (start us, length us, event | category | flops | bytes accessed | tf_op | source)
XLA Modules:
  0.0 91.6 jit_solution(15522334329099085879)
XLA Ops:
  0.0 86.5 %layer.1 = f32[2048,512]{1,0:T(8,128)} custom-call(bf16[8,16,16,512]{3,2,1,0:T(8,128)(2,1)} %cells.1, s32[8,16,16]{2,1,0:T(8,128)} %mask.1, f32[27,512]{1,0:T(8,128)} %conv.1, bf16[1024,512]{1,0:T(8,128)(2,1)} %rest_0_.1, bf16[512,512]{1,0:T(8,128)(2,1)} %rest_1_.1, bf16[512,512]{1,0:T(8,128)(2,1)} %rest_2_.1, bf16[512,512]{1,0:T(8,128)(2,1)} %rest_3_.1, ...), custom_call_target="tpu_custom_call" | custom-call | tf_op jit(solution)/shard_map/layer/pallas_call | solution.py:469
  86.5 5.0 %copy.14 = f32[8,16,16,512]{3,2,1,0:T(8,128)} copy(f32[8,16,16,512]{3,2,1,0:T(8,128)} %bitcast.1) | data formatting | bytes 8388608

commit v4 on v3

--- a/solution.py
+++ b/solution.py
@@ -56,7 +56,7 @@
     latents, w_q1, w_k1, w_v1, w_q2, w_o1, w_k2, w_v2, w_o2 = rest[10:19]
     (
     masked, x_side, y_side, corner, pad, taps, mixed, q1, k1, v1, q2,
-    part, stat, part_in, stat_in, group, group_in, own, gathered, sums, tops, staged,
+    part, stat, part_in, stat_in, group, group_in, own, gathered, sums, tops,
     send_side, recv_side,
     send_part, recv_part, send_stat, recv_stat, send_group, recv_group,
     send_own, recv_own, send_read, recv_read, load_sem, store_sem,
@@ -217,7 +217,7 @@
         load.wait()
     lax.fori_loop(0, 4, project_first, 0)
 
-    def attend(chunk):
+    def attend(chunk, first_pair, last_pair):
         rows = pl.ds(pl.multiple_of(chunk * block, block), block)
 
         def scores(pair, half):
@@ -232,9 +232,9 @@
             summed = dot(weight, values)
             return summed[:, :128] / summed[:, 128:], top * scale + jnp.log2(summed[:, 128:])
 
-        items = [(pair, half) for pair in range(pairs) for half in range(2)]
+        items = [(pair, half) for pair in range(first_pair, last_pair) for half in range(2)]
         found = pipelined(items, scores, weigh, read)
-        for pair in range(pairs):
+        for pair in range(first_pair, last_pair):
             (first, first_log), (second, second_log) = found[(pair, 0)], found[(pair, 1)]
             start = pair * block
             part[chunk, start : start + block, :] = jnp.where(lane < 64, first, second).astype(BF16)
@@ -332,12 +332,8 @@
         lax.fori_loop(1, inner, send, 0)
 
     def turn(step, carry):
-        attend(step)
+        attend(step, 0, pairs)
         send_first(step)
-
-        @pl.when(step >= 3)
-        def _():
-            spread(step - 3)
 
         @pl.when(step >= 2)
         def _():
@@ -349,7 +345,13 @@
 
         return carry
 
-    lax.fori_loop(0, chunks, turn, 0)
+    lax.fori_loop(0, chunks - 1, turn, 0)
+    attend(chunks - 1, 0, pairs - 1)
+    spread(chunks - 4)
+    merge_second(chunks - 3)
+    attend(chunks - 1, pairs - 1, pairs)
+    send_first(chunks - 1)
+    merge_first(chunks - 2)
 
     def latent_side(chunk):
         wait_for(gathered.at[chunk, 1:inner], recv_read.at[chunk])
@@ -362,8 +364,8 @@
     high = cell_count // 4
 
     def leave(step):
-        rows = pl.ds(pl.multiple_of(step * high, high), high)
-        return pltpu.make_async_copy(staged.at[step], out.at[rows], store_sem.at[step])
+        planes = pl.ds(step * (size_x // 4), size_x // 4)
+        return pltpu.make_async_copy(pad.at[planes, 0:size_y], out.at[planes], store_sem.at[step])
 
     def absorb(part_index, keys, values, between):
         last = part_index == 1
@@ -410,7 +412,8 @@
                 score, (weight, shrink) = later, new
             if last:
                 residual = masked[pl.ds(step * per, per)].reshape(high, width).astype(F32)
-                staged[step] = residual + dot(jnp.concatenate(joined, axis=1), w_o2[...])
+                result = residual + dot(jnp.concatenate(joined, axis=1), w_o2[...])
+                pad[pl.ds(step * per, per), 0:size_y] = result.reshape(per, size_y, size_z, width)
                 leave(step).start()
             else:
                 between(step)
@@ -468,7 +471,7 @@
     own_rows = slice_rows // outer
     return pl.pallas_call(
         functools.partial(layer_kernel, scale, chunks),
-        out_shape=jax.ShapeDtypeStruct((count, width), F32),
+        out_shape=jax.ShapeDtypeStruct(cells.shape, F32),
         in_specs=[vmem()] * 3 + [pl.BlockSpec(memory_space=pl.ANY)] * 9,
         out_specs=pl.BlockSpec(memory_space=pl.ANY),
         scratch_shapes=[pltpu.VMEM(array.shape, array.dtype) for array in (latents, *weights)]
@@ -494,7 +497,6 @@
             pltpu.VMEM((chunks, inner, slice_rows, 128), BF16),
             pltpu.VMEM((width // 64, count, 128), F32),
             pltpu.VMEM((width // 64, count, 128), F32),
-            pltpu.VMEM((4, count // 4, width), F32),
         ]
         + [pltpu.SemaphoreType.DMA((8,))] * 2
         + [pltpu.SemaphoreType.DMA((chunks,))] * 10

time: 91.8 us -> 91.4 us (level)
  no operation moved by 1% of the time
where the time goes in v4:
time: 91.4 us; the launch traced here: 91.2 us
  Pallas kernels  86.2 us (94%)
  local copies, waits for them, and re-layouts  5.04 us (6%)
    pallas_call x1, Pallas kernels, layer_call(): pl.pallas_call(functools.partial(layer_kernel, scale, chunks), out_shape=...  86.2 us
    unnamed x1, local copies, waits for them, and re-layouts  5.04 us

profile of v4, /device:TPU:1, one launch (start us, length us, event | category | flops | bytes accessed | tf_op | source)
XLA Modules:
  0.0 91.2 jit_solution(14851133217491760230)
XLA Ops:
  0.0 86.2 %layer.1 = f32[8,16,16,512]{3,2,1,0:T(8,128)} custom-call(bf16[8,16,16,512]{3,2,1,0:T(8,128)(2,1)} %cells.1, s32[8,16,16]{2,1,0:T(8,128)} %mask.1, f32[27,512]{1,0:T(8,128)} %conv.1, bf16[1024,512]{1,0:T(8,128)(2,1)} %rest_0_.1, bf16[512,512]{1,0:T(8,128)(2,1)} %rest_1_.1, bf16[512,512]{1,0:T(8,128)(2,1)} %rest_2_.1, bf16[512,512]{1,0:T(8,128)(2,1)} %rest_3_.1, ...), custom_call_target="tpu_custom_call" | custom-call | tf_op jit(solution)/shard_map/layer/pallas_call | solution.py:472
  86.2 5.0 %copy.14 = f32[8,16,16,512]{3,2,1,0:T(8,128)} copy(f32[8,16,16,512]{3,2,1,0:T(8,128)} %layer.1) | data formatting | bytes 8388608
